TPU v7x, 32 devices: a whole 2x2x4 slice. The times are simulated.
32 devices in a mesh: leaf: 2 (over core), front: 16 (over z, y, x).
Axes of the slice: x: 2, y: 2, z: 4, core: 2. Of those that a mesh axis runs over, the one named last changes fastest.
Arguments:
- front_block: float32 [8192, 8192], P('leaf', 'front'), as said below
- child_update: float32 [2, 6144, 8192], P('leaf', None, 'front'), as said below
- child_map: int32 [2, 48], P('leaf'), may hold values from 0 to 63, as said below
Outputs:
- factored: float32 [8192, 8192], P('leaf', 'front')
Inputs may be any that keep to these rules, and one draw needn't show every extreme that they name: `child_map`: each row is strictly increasing, holds 48 distinct blocks, and always names block 0 and block 63. `front_block`: Symmetric; the assembled front is positive definite. `child_update`: each child's update is symmetric and positive semidefinite in the child's order; columns of parent blocks that the child's map does not name are zero.
All inputs are finite; a program needn't handle non-finite values.
Results may differ from a plain program's by a relative error of at most 0.000088.
Values sent between devices are 32-bit elements; how exact they have to be, the bound alone decides.
No kernel may reach another device: no remote copies, remote signals or barrier semaphores. Data moves between devices by JAX's collectives and lax.ppermute only.
A program may use at most 128 MiB of HBM per device.

v0:
```python
import functools

import jax
import jax.numpy as jnp
from jax import lax
from jax.experimental import pallas as pl
from jax.experimental.pallas import tpu as pltpu
from jax.sharding import PartitionSpec as P

BLK = 128
S = 512
SUB = 8
MIB = 1024 * 1024


def lane_spread(tile, lane):
    return jnp.broadcast_to(tile[:, lane:lane + 1], tile.shape)


def row_spread(tile, row):
    return jnp.broadcast_to(tile[row:row + 1, :], tile.shape)


def eliminate_block(block):
    strips = BLK // SUB
    sub = lax.broadcasted_iota(jnp.int32, (SUB, BLK), 0)
    lane = lax.broadcasted_iota(jnp.int32, (SUB, BLK), 1)
    upper = [block[SUB * s:SUB * s + SUB, :] for s in range(strips)]
    lower = [jnp.where(lane == sub + SUB * s, 1.0, 0.0) for s in range(strips)]
    pivots = []
    for p in range(strips):
        first = SUB * p
        cols = [lane_spread(upper[p], first + j) for j in range(SUB)]
        a, x = upper[p], lower[p]
        recips = []
        pivot = jnp.zeros((SUB, BLK), jnp.float32)
        for j in range(SUB):
            d = row_spread(cols[j], j)
            recip = 1.0 / d
            recips.append(recip)
            pivot = jnp.where(sub == j, d, pivot)
            if j + 1 < SUB:
                m = jnp.where(sub > j, cols[j] * recip, 0.0)
                for k in range(j + 1, SUB):
                    cols[k] = cols[k] - m * row_spread(cols[k], j)
                a = a - m * row_spread(a, j)
                x = x - m * row_spread(x, j)
        upper[p], lower[p] = a, x
        pivots.append(pivot)
        if p + 1 == strips:
            break
        va = [row_spread(a, j) * recips[j] for j in range(SUB)]
        vx = [row_spread(x, j) * recips[j] for j in range(SUB)]
        for j in range(SUB - 2, -1, -1):
            for k in range(j + 1, SUB):
                c = row_spread(cols[k], j) * recips[j]
                va[j] = va[j] - c * va[k]
                vx[j] = vx[j] - c * vx[k]
        for s in range(p + 1, strips):
            b = [lane_spread(upper[s], first + j) for j in range(SUB)]
            upper[s] = upper[s] - (
                ((b[0] * va[0] + b[1] * va[1]) + (b[2] * va[2] + b[3] * va[3]))
                + ((b[4] * va[4] + b[5] * va[5]) + (b[6] * va[6] + b[7] * va[7]))
            )
            lower[s] = lower[s] - (
                ((b[0] * vx[0] + b[1] * vx[1]) + (b[2] * vx[2] + b[3] * vx[3]))
                + ((b[4] * vx[4] + b[5] * vx[5]) + (b[6] * vx[6] + b[7] * vx[7]))
            )
    return (
        jnp.concatenate(upper, axis=0),
        jnp.concatenate(lower, axis=0),
        jnp.concatenate(pivots, axis=0),
    )


def exact_dot(a, b, dims=((1,), (0,))):
    return lax.dot_general(
        a, b, (dims, ((), ())),
        precision=lax.Precision.HIGHEST,
        preferred_element_type=jnp.float32,
    )


def vmem_specs(count):
    return [pl.BlockSpec(memory_space=pltpu.VMEM)] * count


def pivot_rows_kernel(place, blocks, front_hbm, child_hbm, out_ref, front_ref, child_ref, sems):
    def copies(b):
        rows = slice(b * BLK, (b + 1) * BLK)
        return [
            pltpu.make_async_copy(hbm.at[rows, :], ref.at[rows, :], sems.at[n, b])
            for n, (hbm, ref) in enumerate(((front_hbm, front_ref), (child_hbm, child_ref)))]

    waits = [copies(b) for b in range(S // BLK)]
    for pair in waits:
        for copy in pair:
            copy.start()
    for b in range(S // BLK):
        for copy in waits[b]:
            copy.wait()
        rows = slice(b * BLK, (b + 1) * BLK)
        total = jnp.where(place[1] == 0, front_ref[rows, :], 0.0)
        for k in range(b + 1):
            total += jnp.where(blocks[k] == b, child_ref[k * BLK:(k + 1) * BLK, :], 0.0)
        out_ref[rows, :] = total


def pivot_rows(place, blocks, front, child):
    cc = front.shape[1]
    smem = pl.BlockSpec(memory_space=pltpu.SMEM)
    hbm = pl.BlockSpec(memory_space=pl.ANY)
    return pl.pallas_call(
        pivot_rows_kernel,
        out_shape=jax.ShapeDtypeStruct((S, cc), jnp.float32),
        in_specs=[smem, smem, hbm, hbm],
        out_specs=pl.BlockSpec(memory_space=pltpu.VMEM),
        scratch_shapes=[pltpu.VMEM((S, cc), jnp.float32)] * 2
        + [pltpu.SemaphoreType.DMA((2, S // BLK))],
        compiler_params=pltpu.CompilerParams(vmem_limit_bytes=54 * MIB),
        cost_estimate=pl.CostEstimate(
            flops=4 * S * cc, bytes_accessed=12 * S * cc, transcendentals=0),
        name="pivot_rows",
    )(place, blocks, front, child)


def child_rows_kernel(pieces, leaf, child_hbm, out_hbm, rows_ref, in_sems, out_sems):
    rows = out_hbm.shape[0]
    size = rows // pieces
    first = (1 - leaf[0]) * (child_hbm.shape[0] - rows)

    def in_copy(n):
        start = pl.multiple_of(first + n * size, BLK)
        return pltpu.make_async_copy(
            child_hbm.at[pl.ds(start, size), :], rows_ref.at[n], in_sems.at[n])

    def out_copy(n):
        return pltpu.make_async_copy(
            rows_ref.at[n], out_hbm.at[n * size:(n + 1) * size, :], out_sems.at[n])

    for n in range(pieces):
        in_copy(n).start()
    for n in range(pieces):
        in_copy(n).wait()
        out_copy(n).start()
    for n in range(pieces):
        out_copy(n).wait()


def child_rows(leaf, child, rows):
    pieces = 8
    hbm = pl.BlockSpec(memory_space=pl.ANY)
    return pl.pallas_call(
        functools.partial(child_rows_kernel, pieces),
        out_shape=jax.ShapeDtypeStruct((rows, child.shape[1]), jnp.float32),
        in_specs=[pl.BlockSpec(memory_space=pltpu.SMEM), hbm],
        out_specs=hbm,
        scratch_shapes=[pltpu.VMEM((pieces, rows // pieces, child.shape[1]), jnp.float32)]
        + [pltpu.SemaphoreType.DMA((pieces,))] * 2,
        compiler_params=pltpu.CompilerParams(vmem_limit_bytes=56 * MIB),
        cost_estimate=pl.CostEstimate(flops=0, bytes_accessed=4 * S, transcendentals=0),
        name="child_rows",
    )(leaf.reshape(1), child)


def packed_blocks():
    count = S // BLK
    order = [(i, j) for i in range(count) for j in range(i, count)]
    return order[:len(order) // 2], order[len(order) // 2:]


def block_slices(block):
    i, j = block
    return slice(i * BLK, (i + 1) * BLK), slice(j * BLK, (j + 1) * BLK)


def pivot_sum_kernel(place, mine_ref, other_ref, cols_ref, piece_ref, *packed):
    cols = mine_ref[...] + other_ref[...]
    cols_ref[...] = cols
    piece_ref[...] = cols.T
    if packed:
        size = packed[0].shape[0]
        for n, blocks in enumerate(zip(*packed_blocks())):
            low, high = (cols[block_slices(block)] for block in blocks)
            value = jnp.where(place[1] == 0, low, high)
            value = jnp.where(place[0] == 0, value, 0.0)
            for ref, start in zip(packed, (0, size)):
                begin = max(n * BLK, start)
                end = min((n + 1) * BLK, start + size)
                if begin < end:
                    ref[begin - start:end - start, :] = value[begin - n * BLK:end - n * BLK]


def pivot_sum(place, mine, other):
    cc = mine.shape[1]
    shapes = [(S, cc), (cc, S)]
    if cc == S:
        shapes += [(len(packed_blocks()[0]) * BLK // 2, BLK)] * 2
    return pl.pallas_call(
        pivot_sum_kernel,
        out_shape=[jax.ShapeDtypeStruct(shape, jnp.float32) for shape in shapes],
        in_specs=[pl.BlockSpec(memory_space=pltpu.SMEM)] + vmem_specs(2),
        out_specs=vmem_specs(len(shapes)),
        compiler_params=pltpu.CompilerParams(vmem_limit_bytes=16 * MIB),
        cost_estimate=pl.CostEstimate(
            flops=S * cc, bytes_accessed=16 * S * cc, transcendentals=0),
        name="pivot_sum",
    )(place, mine, other)


def factor_step(step, u_ref, x_ref):
    rows = slice(step * BLK, (step + 1) * BLK)
    done, rest = slice(0, (step + 1) * BLK), slice((step + 1) * BLK, S)
    block, inverse, pivots = eliminate_block(u_ref[rows, rows])
    scale = lax.rsqrt(pivots)
    scale = scale * (1.5 - 0.5 * pivots * scale * scale)
    r = lax.broadcasted_iota(jnp.int32, (BLK, BLK), 0)
    c = lax.broadcasted_iota(jnp.int32, (BLK, BLK), 1)
    u_ref[rows, rows] = jnp.where(c >= r, block * scale, 0.0)
    inverse = inverse * scale
    x = exact_dot(inverse, x_ref[rows, done])
    x_ref[rows, done] = x
    if step:
        u_ref[rows, :step * BLK] = jnp.zeros((BLK, step * BLK), jnp.float32)
    if step + 1 < S // BLK:
        u = exact_dot(inverse, u_ref[rows, rest])
        u_ref[rows, rest] = u
        u_ref[rest, rest] -= exact_dot(u, u, ((0,), (0,)))
        x_ref[rest, done] -= exact_dot(u, x, ((0,), (0,)))


def first_step_kernel(place, *refs):
    u_ref, x_ref = refs[-2:]
    sources = refs[:-2]
    if len(sources) == 1:
        u_ref[...] = sources[0][...]
    else:
        mine = jnp.concatenate([ref[...] for ref in sources[:2]], axis=0)
        other = jnp.concatenate([ref[...] for ref in sources[2:]], axis=0)
        values = [
            jnp.where(place[1] == 0, mine, other), jnp.where(place[1] == 0, other, mine)]
        for value, blocks in zip(values, packed_blocks()):
            for n, block in enumerate(blocks):
                u_ref[block_slices(block)] = value[n * BLK:(n + 1) * BLK]
    eye = lax.broadcasted_iota(jnp.int32, (S, S), 0) == lax.broadcasted_iota(
        jnp.int32, (S, S), 1)
    x_ref[...] = jnp.where(eye, 1.0, 0.0)
    factor_step(0, u_ref, x_ref)


def middle_step_kernel(step, u_in, x_in, u_ref, x_ref):
    u_ref[...] = u_in[...]
    x_ref[...] = x_in[...]
    factor_step(step, u_ref, x_ref)


def last_step_kernel(place, u_in, x_in, cols_ref, top_ref, mult_ref, u_ref, x_ref):
    u_ref[...] = u_in[...]
    x_ref[...] = x_in[...]
    factor_step(S // BLK - 1, u_ref, x_ref)
    cc = cols_ref.shape[1]
    is_pivot = place[0] < S // cc
    start = pl.multiple_of(jnp.minimum(place[0], S // cc - 1) * cc, cc)
    solved = exact_dot(x_ref[...], cols_ref[...])
    top_ref[...] = jnp.where(is_pivot, u_ref[pl.ds(start, cc), :].T, solved)
    unit = lax.broadcasted_iota(jnp.int32, (S, cc), 0) == start + lax.broadcasted_iota(
        jnp.int32, (S, cc), 1)
    right = jnp.where(is_pivot, jnp.where(unit, -1.0, 0.0), solved)
    mult_ref[...] = exact_dot(x_ref[...], right, ((0,), (0,)))


FACTOR_PARAMS = dict(
    compiler_params=pltpu.CompilerParams(vmem_limit_bytes=48 * MIB),
    cost_estimate=pl.CostEstimate(
        flops=10 ** 6, bytes_accessed=4 * S, transcendentals=0),
)
SQUARE = jax.ShapeDtypeStruct((S, S), jnp.float32)


def first_step(place, sources):
    return pl.pallas_call(
        first_step_kernel,
        out_shape=[SQUARE] * 2,
        in_specs=[pl.BlockSpec(memory_space=pltpu.SMEM)] + vmem_specs(len(sources)),
        out_specs=vmem_specs(2),
        name="factor_step",
        **FACTOR_PARAMS,
    )(place, *sources)


def middle_step(step, u, x):
    return pl.pallas_call(
        functools.partial(middle_step_kernel, step),
        out_shape=[SQUARE] * 2,
        in_specs=vmem_specs(2),
        out_specs=vmem_specs(2),
        name="factor_step",
        **FACTOR_PARAMS,
    )(u, x)


def last_step(place, u, x, cols):
    return pl.pallas_call(
        last_step_kernel,
        out_shape=[jax.ShapeDtypeStruct(cols.shape, jnp.float32)] * 2,
        in_specs=[pl.BlockSpec(memory_space=pltpu.SMEM)] + vmem_specs(3),
        out_specs=vmem_specs(2),
        scratch_shapes=[pltpu.VMEM((S, S), jnp.float32)] * 2,
        name="factor_and_solve",
        **FACTOR_PARAMS,
    )(place, u, x, cols)


GROUP = 4


def assemble_kernel(index, front_hbm, child_hbm, out_hbm, rows_ref, own_ref, *sems):
    front_sems, own_sems, out_sems = sems
    count = rows_ref.shape[0]
    size = GROUP * BLK

    def front_copy(n):
        return pltpu.make_async_copy(
            front_hbm.at[n * size:(n + 1) * size, :], rows_ref.at[n], front_sems.at[n])

    def own_copy(block):
        start = pl.multiple_of(index[0, block] * BLK, BLK)
        return pltpu.make_async_copy(
            child_hbm.at[pl.ds(start, BLK), :], own_ref.at[block], own_sems.at[block])

    def out_copy(n):
        return pltpu.make_async_copy(
            rows_ref.at[n], out_hbm.at[n * size:(n + 1) * size, :], out_sems.at[n])

    for n in range(count):
        front_copy(n).start()
        for j in range(GROUP):
            own_copy(n * GROUP + j).start()
    for n in range(count):
        front_copy(n).wait()
        for j in range(GROUP):
            block = n * GROUP + j
            own_copy(block).wait()
            rows = slice(j * BLK, (j + 1) * BLK)
            rows_ref[n, rows, :] += jnp.where(index[1, block] > 0, own_ref[block], 0.0)
        out_copy(n).start()
    for n in range(count):
        out_copy(n).wait()


def assemble(index, front, child):
    rows, cc = front.shape
    blocks = rows // BLK
    count = blocks // GROUP
    hbm = pl.BlockSpec(memory_space=pl.ANY)
    return pl.pallas_call(
        assemble_kernel,
        out_shape=jax.ShapeDtypeStruct((rows, cc), jnp.float32),
        in_specs=[pl.BlockSpec(memory_space=pltpu.SMEM), hbm, hbm],
        out_specs=hbm,
        scratch_shapes=[
            pltpu.VMEM((count, GROUP * BLK, cc), jnp.float32),
            pltpu.VMEM((blocks, BLK, cc), jnp.float32),
            pltpu.SemaphoreType.DMA((count,)),
            pltpu.SemaphoreType.DMA((blocks,)),
            pltpu.SemaphoreType.DMA((count,)),
        ],
        compiler_params=pltpu.CompilerParams(vmem_limit_bytes=52 * MIB),
        cost_estimate=pl.CostEstimate(
            flops=rows, bytes_accessed=16 * rows, transcendentals=0),
        name="assemble",
    )(index, front, child)


def finish_kernel(parts, place, index, base_hbm, recv_hbm, mult_ref, top_ref, *refs):
    pieces, refs = refs[:len(parts)], refs[len(parts):]
    out_hbm, rows_ref, piece_ref, recv_ref, base_sems, piece_sems, recv_sems, out_sems = refs
    cc = mult_ref.shape[1]
    is_pivot = place[0] < S // cc

    def start_of(n):
        slot, first, _ = parts[n]
        return pl.multiple_of(jnp.bitwise_xor(place[2], slot) * cc + first, parts[n][2])

    def held(ref, n):
        return ref.at[n, pl.ds(0, parts[n][2]), :]

    def rows_of(n):
        return pl.ds(start_of(n), parts[n][2])

    def base_copy(n):
        return pltpu.make_async_copy(base_hbm.at[rows_of(n), :], held(rows_ref, n), base_sems.at[n])

    def piece_copy(n):
        return pltpu.make_async_copy(pieces[n], held(piece_ref, n), piece_sems.at[n])

    def recv_copy(n, j, size):
        block = (start_of(n) + j) // BLK
        start = pl.multiple_of(index[2, block] * BLK + (parts[n][1] + j) % BLK, size)
        return pltpu.make_async_copy(
            recv_hbm.at[pl.ds(start, size), :], recv_ref.at[n, pl.ds(j, size), :],
            recv_sems.at[n, j // size])

    def out_copy(n):
        return pltpu.make_async_copy(held(rows_ref, n), out_hbm.at[rows_of(n), :], out_sems.at[n])

    def pieces_of(n):
        size = min(BLK, parts[n][2])
        return [(j, size) for j in range(0, parts[n][2], size)]

    for n in range(len(parts)):
        piece_copy(n).start()
        base_copy(n).start()
        for j, size in pieces_of(n):
            recv_copy(n, j, size).start()
    for n in range(len(parts)):
        piece_copy(n).wait()
        base_copy(n).wait()
        for j, size in pieces_of(n):
            recv_copy(n, j, size).wait()
        is_top = jnp.logical_and(place[1] == 0, start_of(n) < S)

        @pl.when(is_top)
        def _():
            held(rows_ref, n)[...] = top_ref[rows_of(n), :]

        @pl.when(jnp.logical_not(is_top))
        def _():
            product = lax.dot_general(
                held(piece_ref, n)[...], mult_ref[...], (((1,), (0,)), ((), ())),
                precision=lax.Precision.HIGH,
                preferred_element_type=jnp.float32,
            )
            for j, size in pieces_of(n):
                there = index[3, (start_of(n) + j) // BLK] > 0
                rows = pl.ds(j, size)
                base = rows_ref[n, rows, :] + jnp.where(there, recv_ref[n, rows, :], 0.0)
                rows_ref[n, rows, :] = jnp.where(is_pivot, 0.0, base) - product[j:j + size, :]

        out_copy(n).start()
    for n in range(len(parts)):
        out_copy(n).wait()


def finish(place, index, base, recv, parts, mult, top):
    rows, cc = base.shape
    count = len(parts)
    total = sum(piece.shape[0] for _, _, piece in parts)
    hbm = pl.BlockSpec(memory_space=pl.ANY)
    smem = pl.BlockSpec(memory_space=pltpu.SMEM)
    keys = tuple((slot, first, piece.shape[0]) for slot, first, piece in parts)
    return pl.pallas_call(
        functools.partial(finish_kernel, keys),
        out_shape=jax.ShapeDtypeStruct((rows, cc), jnp.float32),
        in_specs=[smem, smem, hbm, hbm] + vmem_specs(2) + [hbm] * count,
        out_specs=hbm,
        scratch_shapes=[
            pltpu.VMEM((count, cc, cc), jnp.float32),
            pltpu.VMEM((count, cc, S), jnp.float32),
            pltpu.VMEM((count, cc, cc), jnp.float32),
            pltpu.SemaphoreType.DMA((count,)),
            pltpu.SemaphoreType.DMA((count,)),
            pltpu.SemaphoreType.DMA((count, -(-cc // BLK))),
            pltpu.SemaphoreType.DMA((count,)),
        ],
        input_output_aliases={2: 0},
        compiler_params=pltpu.CompilerParams(vmem_limit_bytes=48 * MIB),
        cost_estimate=pl.CostEstimate(
            flops=6 * total * S * cc, bytes_accessed=4 * total * (3 * cc + S),
            transcendentals=0),
        name="finish",
    )(place, index, base, recv, mult, top, *[piece for _, _, piece in parts])


def block_places(blocks, first, count, shift, limit):
    parent = first + jnp.arange(count, dtype=jnp.int32)
    reached = jnp.sum((blocks[None, :] <= parent[:, None]).astype(jnp.int32), axis=1)
    there = jnp.sum((blocks[None, :] == parent[:, None]).astype(jnp.int32), axis=1)
    return jnp.clip(reached - 1 - shift, 0, limit - 1), there


def spread_pivot(cols, front_index, front_count, holders):
    leaf_index = lax.axis_index("leaf")
    half = S // 2
    mine = lax.dynamic_slice_in_dim(cols, leaf_index * half, half, 0)
    steps = []
    step = holders
    while step < front_count:
        steps.append(step)
        step *= 2
    pieces = []
    for order, part in ((steps, mine[:half // 2]), (steps[::-1], mine[half // 2:])):
        held = list(range(holders))
        part = jnp.where(front_index < holders, part, 0.0)
        for step in order:
            got = lax.ppermute(part, "front", [(f, f + step) for f in held])
            part = part + got
            held += [f + step for f in held]
        pieces.append(part)
    mine = jnp.concatenate(pieces, axis=0)
    if holders > 1:
        groups = [list(range(f, f + holders)) for f in range(0, front_count, holders)]
        mine = lax.all_gather(mine, "front", axis_index_groups=groups, axis=1, tiled=True)
    other = lax.ppermute(mine, "leaf", [(0, 1), (1, 0)])
    low = jnp.where(leaf_index == 0, mine, other)
    high = jnp.where(leaf_index == 0, other, mine)
    return jnp.concatenate([low, high], axis=0)


def pass_on(part, steps, n):
    held = [0]
    for step in steps[:n]:
        held += [f + step for f in held]
    return part + lax.ppermute(part, "front", [(f, f + steps[n]) for f in held])


def per_device(front_block, child_update, child_map):
    row_count, col_count = front_block.shape
    front_count = lax.axis_size("front")
    leaf_index = lax.axis_index("leaf")
    front_index = lax.axis_index("front")
    half = front_count // 2
    place = jnp.stack([front_index, leaf_index, front_index % half]).astype(jnp.int32)
    swap = [(0, 1), (1, 0)]
    child = child_update[0]
    blocks = child_map[0]
    child_blocks = blocks.shape[0]
    parent_blocks = row_count // BLK

    mine = pivot_rows(place, blocks, front_block, child)
    cols, piece, *packed = pivot_sum(place, mine, lax.ppermute(mine, "leaf", swap))

    pairs = [(f, f + half) for f in range(half)]
    pairs += [(front_count + f + half, front_count + f) for f in range(half)]
    came = lax.ppermute(piece, ("leaf", "front"), pairs)

    other_blocks = lax.ppermute(blocks, "leaf", swap)
    first = leaf_index * parent_blocks
    shift = leaf_index * (child_blocks - parent_blocks)
    index = jnp.stack(
        block_places(blocks, first, parent_blocks, 0, child_blocks)
        + block_places(other_blocks, first, parent_blocks, shift, parent_blocks))

    def across(value, bit):
        return lax.ppermute(value, "front", [(f, f ^ bit) for f in range(front_count)])

    barrier = lax.optimization_barrier
    own = (front_index >= half) == (leaf_index == 1)
    if packed:
        orders, step = [[1, 2], [2, 1]], 4
        while step <= half:
            for order in orders:
                order.append(step)
            step *= 2
        parts = [pass_on(part, order, 0) for part, order in zip(packed, orders)]
        parts, later = barrier((parts, leaf_index))
        sent = child_rows(later, child, row_count)
        parts = [pass_on(part, order, 1) for part, order in zip(parts, orders)]
        parts, sent, index = barrier((parts, sent, index))
        base = assemble(index, front_block, child)
        for n in range(2, len(orders[0]) - 1):
            parts = [pass_on(part, order, n) for part, order in zip(parts, orders)]
        parts, came, base = barrier((parts, came, base))
    else:
        sent = child_rows(leaf_index, child, row_count)
        base = assemble(index, front_block, child)
        sources = [spread_pivot(cols, front_index, front_count, S // col_count)]
    piece = jnp.where(own, piece, came)

    bit, slots, held = half // 2, [0], [piece]
    while bit > 4:
        held += [across(part, bit) for part in held]
        slots += [slot + bit for slot in slots]
        bit //= 2
    sides = [(across(part, 1), across(part, 2)) for part in held]
    if packed:
        parts = [pass_on(part, order, len(order) - 1) for part, order in zip(parts, orders)]
        parts, held = barrier((parts, held))
        sources = parts + [lax.ppermute(part, "leaf", swap) for part in parts]
    over = [across(part, 4) for part in held]
    sources, sides = barrier((sources, sides))
    cut = col_count // 2
    crossed = [(across(xs[:cut], 2), across(ys[cut:], 1)) for xs, ys in sides]
    u, x = first_step(place, sources)
    u, x = middle_step(1, u, x)
    u, x, over, crossed, sent = barrier((u, x, over, crossed, sent))
    recv = lax.ppermute(sent, "leaf", swap)
    over_sides = [(across(part, 1), across(part, 2)) for part in over]
    over_crossed = [(across(low, 4), across(high, 4)) for low, high in crossed]
    u, x = middle_step(2, u, x)
    top, mult = last_step(place, u, x, cols)

    early, late = [], []
    for group, first, alone, beside, cross in (
            (early, 0, held, sides, crossed), (late, 4, over, over_sides, over_crossed)):
        for slot, part, (xs, ys), (low, high) in zip(slots, alone, beside, cross):
            slot += first
            early.append((slot, 0, part))
            group += [(slot + 1, 0, xs), (slot + 2, 0, ys)]
            group += [(slot + 3, 0, low), (slot + 3, cut, high)]
    for group in (early, late):
        base = finish(place, index, base, recv, group, mult, top)
    return base


def solution(mesh):
    return jax.shard_map(
        per_device,
        mesh=mesh,
        in_specs=(P("leaf", "front"), P("leaf", None, "front"), P("leaf", None)),
        out_specs=P("leaf", "front"),
        check_vma=False,
    )
```

profile of v0, /device:TPU:0, one launch (start us, length us, event | category | flops | bytes accessed | tf_op | source)
XLA Modules:
  0.0 132.7 jit_solution(8077703401178516824)
XLA Ops:
  0.6 3.4 %pivot_rows.1.mine_ref = f32[512,512]{1,0:T(8,128)} custom-call(s32[3]{0:T(128)} %pad_add_fusion.1.place, s32[48]{0:T(128)} %bitcast.15, f32[4096,512]{1,0:T(8,128)} %front_hbm.3, f32[6144,512]{1,0:T(8,128)} %bitcast.12), custom_call_target="tpu_custom_call" | custom-call | flops 1048576 | bytes 3145728 | tf_op jit(solution)/shard_map/pivot_rows/pallas_call | solution.py:113
  4.6 2.5 %collective-permute-done.other_ref = f32[512,512]{1,0:T(8,128)S(1)} collective-permute-done((f32[512,512]{1,0:T(8,128)}, f32[512,512]{1,0:T(8,128)S(1)}, u32[]{:S(2)}, u32[]{:S(2)}) %collective-permute-start) | collective-permute-done | bytes 1048608 | tf_op jit(solution)/shard_map/ppermute | solution.py:531
  9.2 5.9 %collective-permute-start.8 = (f32[512,512]{1,0:T(8,128)S(1)}, f32[512,512]{1,0:T(8,128)S(1)}, u32[]{:S(2)}, u32[]{:S(2)}) collective-permute-start(f32[512,512]{1,0:T(8,128)S(1)} %get-tuple-element.51), channel_id=1, source_target_pairs={{0,8},{1,9},{2,10},{3,11},{4,12},{5,13},{6,14},{7,15},{24,16},{25,... | collective-permute-start | bytes 3145736 | tf_op jit(solution)/shard_map/ppermute | solution.py:535
  16.5 3.4 %collective-permute-start.2 = (f32[320,128]{1,0:T(8,128)S(1)}, f32[320,128]{1,0:T(8,128)S(1)}, u32[]{:S(2)}, u32[]{:S(2)}) collective-permute-start(f32[320,128]{1,0:T(8,128)S(1)} %get-tuple-element.44), channel_id=1, source_target_pairs={{0,2},{16,18}} | collective-permute-start | bytes 491528 | tf_op jit(solution)/shard_map/ppermute | solution.py:514
  20.0 1.3 collective-permute-start.1
  21.3 2.5 %collective-permute-done.2 = f32[320,128]{1,0:T(8,128)S(1)} collective-permute-done((f32[320,128]{1,0:T(8,128)S(1)}, f32[320,128]{1,0:T(8,128)S(1)}, u32[]{:S(2)}, u32[]{:S(2)}) %collective-permute-start.2) | collective-permute-done | bytes 163872 | tf_op jit(solution)/shard_map/ppermute | solution.py:514
  25.1 4.4 %collective-permute-start.4 = (f32[320,128]{1,0:T(8,128)S(1)}, f32[320,128]{1,0:T(8,128)S(1)}, u32[]{:S(2)}, u32[]{:S(2)}) collective-permute-start(f32[320,128]{1,0:T(8,128)S(1)} %add.60), channel_id=1, source_target_pairs={{0,1},{2,3},{16,17},{18,19}} | collective-permute-start | bytes 491528 | tf_op jit(solution)/shard_map/ppermute | solution.py:514
  30.9 6.5 %child_rows.1 = f32[4096,512]{1,0:T(8,128)} custom-call(s32[1]{0:T(128)} %bitcast.5.leaf, f32[6144,512]{1,0:T(8,128)} %bitcast.13), custom_call_target="tpu_custom_call" | custom-call | bytes 2048 | tf_op jit(solution)/shard_map/child_rows/pallas_call | solution.py:153
  37.4 2.0 %collective-permute-start.7 = (f32[320,128]{1,0:T(8,128)S(1)}, f32[320,128]{1,0:T(8,128)}, u32[]{:S(2)}, u32[]{:S(2)}) collective-permute-start(f32[320,128]{1,0:T(8,128)S(1)} %add.62), channel_id=1, source_target_pairs={{0,4},{2,6},{1,5},{3,7},{16,20},{18,22},{17,21},{19,23}} | collective-permute-start | bytes 491528 | tf_op jit(solution)/shard_map/ppermute | solution.py:514
  39.4 1.9 %collective-permute-start.6 = (f32[320,128]{1,0:T(8,128)S(1)}, f32[320,128]{1,0:T(8,128)}, u32[]{:S(2)}, u32[]{:S(2)}) collective-permute-start(f32[320,128]{1,0:T(8,128)S(1)} %add.61), channel_id=1, source_target_pairs={{0,4},{1,5},{2,6},{3,7},{16,20},{17,21},{18,22},{19,23}} | collective-permute-start | bytes 491528 | tf_op jit(solution)/shard_map/ppermute | solution.py:514
  41.4 9.9 %assemble.1.base_hbm = f32[4096,512]{1,0:T(8,128)} custom-call(s32[4,32]{1,0:T(4,128)S(1)} %pad_add_fusion.index, f32[4096,512]{1,0:T(8,128)} %front_hbm.3, f32[6144,512]{1,0:T(8,128)} %bitcast.14), custom_call_target="tpu_custom_call" | custom-call | flops 4096 | bytes 65536 | tf_op jit(solution)/shard_map/assemble/pallas_call | solution.py:356
  54.9 1.5 %collective-permute-start.9 = (f32[320,128]{1,0:T(8,128)S(1)}, f32[320,128]{1,0:T(8,128)S(1)}, u32[]{:S(2)}, u32[]{:S(2)}) collective-permute-start(f32[320,128]{1,0:T(8,128)S(1)} %add.65), channel_id=1, source_target_pairs={{0,8},{1,9},{2,10},{3,11},{4,12},{5,13},{6,14},{7,15},{16,24},{17,... | collective-permute-start | bytes 491528 | tf_op jit(solution)/shard_map/ppermute | solution.py:514
  56.4 3.1 %collective-permute-done.10 = f32[320,128]{1,0:T(8,128)S(1)} collective-permute-done((f32[320,128]{1,0:T(8,128)S(1)}, f32[320,128]{1,0:T(8,128)S(1)}, u32[]{:S(2)}, u32[]{:S(2)}) %collective-permute-start.10) | collective-permute-done | bytes 163872 | tf_op jit(solution)/shard_map/ppermute | solution.py:514
  59.5 2.8 %collective-permute-done.9 = f32[320,128]{1,0:T(8,128)S(1)} collective-permute-done((f32[320,128]{1,0:T(8,128)S(1)}, f32[320,128]{1,0:T(8,128)S(1)}, u32[]{:S(2)}, u32[]{:S(2)}) %collective-permute-start.9) | collective-permute-done | bytes 163872 | tf_op jit(solution)/shard_map/ppermute | solution.py:514
  64.6 13.1 %collective-permute-done.13.refs_1_ = f32[512,512]{1,0:T(8,128)S(1)} collective-permute-done((f32[512,512]{1,0:T(8,128)S(1)}, f32[512,512]{1,0:T(8,128)S(1)}, u32[]{:S(2)}, u32[]{:S(2)}) %collective-permute-start.13) | collective-permute-done | bytes 1048608 | tf_op jit(solution)/shard_map/ppermute | solution.py:545
  78.3 1.7 %collective-permute-start.17 = (f32[256,512]{1,0:T(8,128)S(1)}, f32[256,512]{1,0:T(8,128)S(1)}, u32[]{:S(2)}, u32[]{:S(2)}) collective-permute-start(f32[256,512]{1,0:T(8,128)S(1)} %slice.7), channel_id=1, source_target_pairs={{0,1},{1,0},{2,3},{3,2},{4,5},{5,4},{6,7},{7,6},{8,9},{9,8},{10,11... | collective-permute-start | bytes 1572872 | tf_op jit(solution)/shard_map/ppermute | solution.py:545
  80.0 7.3 %factor_step.3 = (f32[512,512]{1,0:T(8,128)S(1)}, f32[512,512]{1,0:T(8,128)S(1)}) custom-call(s32[3]{0:T(128)S(1)} %copy-done.1, f32[320,128]{1,0:T(8,128)S(1)} %add.67.refs_0_, f32[320,128]{1,0:T(8,128)S(1)} %add.68.refs_1_, f32[320,128]{1,0:T(8,128)S(1)} %collective-permute-done.11.refs_2_, f32[320,128]{1,0:T(8,128)S(1)} %collective-permute-done.12.refs_3_), custom_call_target="tpu_custom_call" | custom-call | flops 1000000 | bytes 2048 | tf_op jit(solution)/shard_map/factor_step/pallas_call | solution.py:281
  87.3 6.5 %factor_step.4 = (f32[512,512]{1,0:T(8,128)S(1)}, f32[512,512]{1,0:T(8,128)S(1)}) custom-call(f32[512,512]{1,0:T(8,128)S(1)} %get-tuple-element.62.u_in, f32[512,512]{1,0:T(8,128)S(1)} %get-tuple-element.63.x_in), custom_call_target="tpu_custom_call" | custom-call | flops 1000000 | bytes 2048 | tf_op jit(solution)/shard_map/factor_step/pallas_call | solution.py:292
  94.4 1.7 %collective-permute-start.20 = (f32[512,512]{1,0:T(8,128)S(1)}, f32[512,512]{1,0:T(8,128)S(1)}, u32[]{:S(2)}, u32[]{:S(2)}) collective-permute-start(f32[512,512]{1,0:T(8,128)S(1)} %collective-permute-done.15.refs_5_), channel_id=1, source_target_pairs={{0,2},{1,3},{2,0},{3,1},{4,6},{5,7},{6,4},{7,5},{8,10},{9,11},{10,... | collective-permute-start | bytes 3145736 | tf_op jit(solution)/shard_map/ppermute | solution.py:545
  96.1 2.0 %collective-permute-start.22 = (f32[256,512]{1,0:T(8,128)S(1)}, f32[256,512]{1,0:T(8,128)S(1)}, u32[]{:S(2)}, u32[]{:S(2)}) collective-permute-start(f32[256,512]{1,0:T(8,128)S(1)} %collective-permute-done.17.refs_4_), channel_id=1, source_target_pairs={{0,4},{1,5},{2,6},{3,7},{4,0},{5,1},{6,2},{7,3},{8,12},{9,13},{10,... | collective-permute-start | bytes 1572872 | tf_op jit(solution)/shard_map/ppermute | solution.py:545
  98.1 6.6 %factor_step.5 = (f32[512,512]{1,0:T(8,128)S(1)}, f32[512,512]{1,0:T(8,128)S(1)}) custom-call(f32[512,512]{1,0:T(8,128)S(1)} %get-tuple-element.71.u_in, f32[512,512]{1,0:T(8,128)S(1)} %get-tuple-element.72.x_in), custom_call_target="tpu_custom_call" | custom-call | flops 1000000 | bytes 2048 | tf_op jit(solution)/shard_map/factor_step/pallas_call | solution.py:292
  104.7 10.2 %factor_and_solve.1 = (f32[512,512]{1,0:T(8,128)S(1)}, f32[512,512]{1,0:T(8,128)S(1)}) custom-call(s32[3]{0:T(128)S(1)} %copy-done.1, f32[512,512]{1,0:T(8,128)S(1)} %get-tuple-element.73.u_in, f32[512,512]{1,0:T(8,128)S(1)} %get-tuple-element.74.x_in, f32[512,512]{1,0:T(8,128)S(1)} %get-tuple-element.75.cols_ref), custom_call_target="tpu_custom_call" | custom-call | flops 1000000 | bytes 2048 | tf_op jit(solution)/shard_map/factor_and_solve/pallas_call | solution.py:303
  115.0 10.6 %finish.2.base_hbm = f32[4096,512]{1,0:T(8,128)} custom-call(s32[3]{0:T(128)S(1)} %copy-done.1, s32[4,32]{1,0:T(4,128)S(1)} %pad_add_fusion.index, f32[4096,512]{1,0:T(8,128)} %assemble.1.base_hbm, f32[4096,512]{1,0:T(8,128)} %collective-permute-done.18.recv_hbm, f32[512,512]{1,0:T(8,128)S(1)} %get-tuple-element.76.mult_ref, ...), custom_call_target="tpu_custom_call", output_to_operand_aliasing={{}: (2, {})} | custom-call | flops 4026531840 | bytes 20971520 | tf_op jit(solution)/shard_map/finish/pallas_call | solution.py:452
  125.6 6.9 %finish.3 = f32[4096,512]{1,0:T(8,128)} custom-call(s32[3]{0:T(128)S(1)} %copy-done.1, s32[4,32]{1,0:T(4,128)S(1)} %pad_add_fusion.index, f32[4096,512]{1,0:T(8,128)} %finish.2.base_hbm, f32[4096,512]{1,0:T(8,128)} %collective-permute-done.18.recv_hbm, f32[512,512]{1,0:T(8,128)S(1)} %get-tuple-element.76.mult_ref, ...), custom_call_target="tpu_custom_call", output_to_operand_aliasing={{}: (2, {})} | custom-call | flops 2415919104 | bytes 12582912 | tf_op jit(solution)/shard_map/finish/pallas_call | solution.py:452
  (59 shorter events, 14.2 us)
Async XLA Ops:
  4.0 3.0 %collective-permute-start = (f32[512,512]{1,0:T(8,128)}, f32[512,512]{1,0:T(8,128)S(1)}, u32[]{:S(2)}, u32[]{:S(2)}) collective-permute-start(f32[512,512]{1,0:T(8,128)} %pivot_rows.1.mine_ref), channel_id=1, source_target_pairs={{0,16},{16,0},{1,17},{17,1},{2,18},{18,2},{3,19},{19,3},{4,20},{20... | collective-permute-start | bytes 3145736 | tf_op jit(solution)/shard_map/ppermute | solution.py:531
  9.2 44.0 %collective-permute-start.8 = (f32[512,512]{1,0:T(8,128)S(1)}, f32[512,512]{1,0:T(8,128)S(1)}, u32[]{:S(2)}, u32[]{:S(2)}) collective-permute-start(f32[512,512]{1,0:T(8,128)S(1)} %get-tuple-element.51), channel_id=1, source_target_pairs={{0,8},{1,9},{2,10},{3,11},{4,12},{5,13},{6,14},{7,15},{24,16},{25,... | collective-permute-start | bytes 3145736 | tf_op jit(solution)/shard_map/ppermute | solution.py:535
  15.1 1.2 collective-permute-start.5
  16.5 7.2 %collective-permute-start.2 = (f32[320,128]{1,0:T(8,128)S(1)}, f32[320,128]{1,0:T(8,128)S(1)}, u32[]{:S(2)}, u32[]{:S(2)}) collective-permute-start(f32[320,128]{1,0:T(8,128)S(1)} %get-tuple-element.44), channel_id=1, source_target_pairs={{0,2},{16,18}} | collective-permute-start | bytes 491528 | tf_op jit(solution)/shard_map/ppermute | solution.py:514
  20.0 5.1 %collective-permute-start.1 = (f32[320,128]{1,0:T(8,128)S(1)}, f32[320,128]{1,0:T(8,128)S(1)}, u32[]{:S(2)}, u32[]{:S(2)}) collective-permute-start(f32[320,128]{1,0:T(8,128)S(1)} %get-tuple-element.43), channel_id=1, source_target_pairs={{0,1},{16,17}} | collective-permute-start | bytes 491528 | tf_op jit(solution)/shard_map/ppermute | solution.py:514
  25.1 12.3 %collective-permute-start.4 = (f32[320,128]{1,0:T(8,128)S(1)}, f32[320,128]{1,0:T(8,128)S(1)}, u32[]{:S(2)}, u32[]{:S(2)}) collective-permute-start(f32[320,128]{1,0:T(8,128)S(1)} %add.60), channel_id=1, source_target_pairs={{0,1},{2,3},{16,17},{18,19}} | collective-permute-start | bytes 491528 | tf_op jit(solution)/shard_map/ppermute | solution.py:514
  29.5 7.9 %collective-permute-start.3 = (f32[320,128]{1,0:T(8,128)S(1)}, f32[320,128]{1,0:T(8,128)S(1)}, u32[]{:S(2)}, u32[]{:S(2)}) collective-permute-start(f32[320,128]{1,0:T(8,128)S(1)} %add.59), channel_id=1, source_target_pairs={{0,2},{1,3},{16,18},{17,19}} | collective-permute-start | bytes 491528 | tf_op jit(solution)/shard_map/ppermute | solution.py:514
  37.4 13.8 %collective-permute-start.7 = (f32[320,128]{1,0:T(8,128)S(1)}, f32[320,128]{1,0:T(8,128)}, u32[]{:S(2)}, u32[]{:S(2)}) collective-permute-start(f32[320,128]{1,0:T(8,128)S(1)} %add.62), channel_id=1, source_target_pairs={{0,4},{2,6},{1,5},{3,7},{16,20},{18,22},{17,21},{19,23}} | collective-permute-start | bytes 491528 | tf_op jit(solution)/shard_map/ppermute | solution.py:514
  39.4 12.8 %collective-permute-start.6 = (f32[320,128]{1,0:T(8,128)S(1)}, f32[320,128]{1,0:T(8,128)}, u32[]{:S(2)}, u32[]{:S(2)}) collective-permute-start(f32[320,128]{1,0:T(8,128)S(1)} %add.61), channel_id=1, source_target_pairs={{0,4},{1,5},{2,6},{3,7},{16,20},{17,21},{18,22},{19,23}} | collective-permute-start | bytes 491528 | tf_op jit(solution)/shard_map/ppermute | solution.py:514
  53.4 24.3 %collective-permute-start.13 = (f32[512,512]{1,0:T(8,128)S(1)}, f32[512,512]{1,0:T(8,128)S(1)}, u32[]{:S(2)}, u32[]{:S(2)}) collective-permute-start(f32[512,512]{1,0:T(8,128)S(1)} %broadcast_select_fusion.refs_0_), channel_id=1, source_target_pairs={{0,1},{1,0},{2,3},{3,2},{4,5},{5,4},{6,7},{7,6},{8,9},{9,8},{10,11... | collective-permute-start | bytes 3145736 | tf_op jit(solution)/shard_map/ppermute | solution.py:545
  53.5 24.3 %collective-permute-start.14 = (f32[512,512]{1,0:T(8,128)S(1)}, f32[512,512]{1,0:T(8,128)S(1)}, u32[]{:S(2)}, u32[]{:S(2)}) collective-permute-start(f32[512,512]{1,0:T(8,128)S(1)} %broadcast_select_fusion.refs_0_), channel_id=1, source_target_pairs={{0,2},{1,3},{2,0},{3,1},{4,6},{5,7},{6,4},{7,5},{8,10},{9,11},{10,... | collective-permute-start | bytes 3145736 | tf_op jit(solution)/shard_map/ppermute | solution.py:545
  53.6 5.9 %collective-permute-start.10 = (f32[320,128]{1,0:T(8,128)S(1)}, f32[320,128]{1,0:T(8,128)S(1)}, u32[]{:S(2)}, u32[]{:S(2)}) collective-permute-start(f32[320,128]{1,0:T(8,128)S(1)} %add.66), channel_id=1, source_target_pairs={{0,8},{2,10},{1,9},{3,11},{4,12},{6,14},{5,13},{7,15},{16,24},{18,... | collective-permute-start | bytes 491528 | tf_op jit(solution)/shard_map/ppermute | solution.py:514
  54.9 7.5 %collective-permute-start.9 = (f32[320,128]{1,0:T(8,128)S(1)}, f32[320,128]{1,0:T(8,128)S(1)}, u32[]{:S(2)}, u32[]{:S(2)}) collective-permute-start(f32[320,128]{1,0:T(8,128)S(1)} %add.65), channel_id=1, source_target_pairs={{0,8},{1,9},{2,10},{3,11},{4,12},{5,13},{6,14},{7,15},{16,24},{17,... | collective-permute-start | bytes 491528 | tf_op jit(solution)/shard_map/ppermute | solution.py:514
  62.4 31.5 %collective-permute-start.15 = (f32[512,512]{1,0:T(8,128)S(1)}, f32[512,512]{1,0:T(8,128)S(1)}, u32[]{:S(2)}, u32[]{:S(2)}) collective-permute-start(f32[512,512]{1,0:T(8,128)S(1)} %broadcast_select_fusion.refs_0_), channel_id=1, source_target_pairs={{0,4},{1,5},{2,6},{3,7},{4,0},{5,1},{6,2},{7,3},{8,12},{9,13},{10,... | collective-permute-start | bytes 3145736 | tf_op jit(solution)/shard_map/ppermute | solution.py:545
  63.0 1.4 %collective-permute-start.11 = (f32[320,128]{1,0:T(8,128)S(1)}, f32[320,128]{1,0:T(8,128)S(1)}, u32[]{:S(2)}, u32[]{:S(2)}) collective-permute-start(f32[320,128]{1,0:T(8,128)S(1)} %add.67.refs_0_), channel_id=1, source_target_pairs={{0,16},{16,0},{1,17},{17,1},{2,18},{18,2},{3,19},{19,3},{4,20},{20... | collective-permute-start | bytes 491528 | tf_op jit(solution)/shard_map/ppermute | solution.py:579
  63.0 1.6 %collective-permute-start.12 = (f32[320,128]{1,0:T(8,128)S(1)}, f32[320,128]{1,0:T(8,128)S(1)}, u32[]{:S(2)}, u32[]{:S(2)}) collective-permute-start(f32[320,128]{1,0:T(8,128)S(1)} %add.68.refs_1_), channel_id=1, source_target_pairs={{0,16},{16,0},{1,17},{17,1},{2,18},{18,2},{3,19},{19,3},{4,20},{20... | collective-permute-start | bytes 491528 | tf_op jit(solution)/shard_map/ppermute | solution.py:579
  77.8 37.2 %copy-start.2 = (f32[512,512]{1,0:T(8,128)}, f32[512,512]{1,0:T(8,128)S(1)}, u32[]{:S(2)}) copy-start(f32[512,512]{1,0:T(8,128)S(1)} %collective-permute-done.14.refs_2_) | copy-start | bytes 3145732
  77.9 16.0 %collective-permute-start.16 = (f32[256,512]{1,0:T(8,128)S(1)}, f32[256,512]{1,0:T(8,128)S(1)}, u32[]{:S(2)}, u32[]{:S(2)}) collective-permute-start(f32[256,512]{1,0:T(8,128)S(1)} %slice.6), channel_id=1, source_target_pairs={{0,2},{1,3},{2,0},{3,1},{4,6},{5,7},{6,4},{7,5},{8,10},{9,11},{10,... | collective-permute-start | bytes 1572872 | tf_op jit(solution)/shard_map/ppermute | solution.py:545
  78.3 15.6 %collective-permute-start.17 = (f32[256,512]{1,0:T(8,128)S(1)}, f32[256,512]{1,0:T(8,128)S(1)}, u32[]{:S(2)}, u32[]{:S(2)}) collective-permute-start(f32[256,512]{1,0:T(8,128)S(1)} %slice.7), channel_id=1, source_target_pairs={{0,1},{1,0},{2,3},{3,2},{4,5},{5,4},{6,7},{7,6},{8,9},{9,8},{10,11... | collective-permute-start | bytes 1572872 | tf_op jit(solution)/shard_map/ppermute | solution.py:545
  93.9 21.1 %collective-permute-start.18 = (f32[4096,512]{1,0:T(8,128)}, f32[4096,512]{1,0:T(8,128)}, u32[]{:S(2)}, u32[]{:S(2)}) collective-permute-start(f32[4096,512]{1,0:T(8,128)} %child_rows.1), channel_id=1, source_target_pairs={{0,16},{16,0},{1,17},{17,1},{2,18},{18,2},{3,19},{19,3},{4,20},{20... | collective-permute-start | bytes 25165832 | tf_op jit(solution)/shard_map/ppermute | solution.py:587
  93.9 31.7 %collective-permute-start.19 = (f32[512,512]{1,0:T(8,128)S(1)}, f32[512,512]{1,0:T(8,128)S(1)}, u32[]{:S(2)}, u32[]{:S(2)}) collective-permute-start(f32[512,512]{1,0:T(8,128)S(1)} %collective-permute-done.15.refs_5_), channel_id=1, source_target_pairs={{0,1},{1,0},{2,3},{3,2},{4,5},{5,4},{6,7},{7,6},{8,9},{9,8},{10,11... | collective-permute-start | bytes 3145736 | tf_op jit(solution)/shard_map/ppermute | solution.py:545
  94.4 31.2 %collective-permute-start.20 = (f32[512,512]{1,0:T(8,128)S(1)}, f32[512,512]{1,0:T(8,128)S(1)}, u32[]{:S(2)}, u32[]{:S(2)}) collective-permute-start(f32[512,512]{1,0:T(8,128)S(1)} %collective-permute-done.15.refs_5_), channel_id=1, source_target_pairs={{0,2},{1,3},{2,0},{3,1},{4,6},{5,7},{6,4},{7,5},{8,10},{9,11},{10,... | collective-permute-start | bytes 3145736 | tf_op jit(solution)/shard_map/ppermute | solution.py:545
  96.1 29.5 %collective-permute-start.21 = (f32[256,512]{1,0:T(8,128)S(1)}, f32[256,512]{1,0:T(8,128)S(1)}, u32[]{:S(2)}, u32[]{:S(2)}) collective-permute-start(f32[256,512]{1,0:T(8,128)S(1)} %collective-permute-done.16.refs_3_), channel_id=1, source_target_pairs={{0,4},{1,5},{2,6},{3,7},{4,0},{5,1},{6,2},{7,3},{8,12},{9,13},{10,... | collective-permute-start | bytes 1572872 | tf_op jit(solution)/shard_map/ppermute | solution.py:545
  96.1 29.5 %collective-permute-start.22 = (f32[256,512]{1,0:T(8,128)S(1)}, f32[256,512]{1,0:T(8,128)S(1)}, u32[]{:S(2)}, u32[]{:S(2)}) collective-permute-start(f32[256,512]{1,0:T(8,128)S(1)} %collective-permute-done.17.refs_4_), channel_id=1, source_target_pairs={{0,4},{1,5},{2,6},{3,7},{4,0},{5,1},{6,2},{7,3},{8,12},{9,13},{10,... | collective-permute-start | bytes 1572872 | tf_op jit(solution)/shard_map/ppermute | solution.py:545
  (4 other events, 43.3 us)
where the time goes:
time: 133 us
  Pallas kernels  68.8 us (52%)
  starting transfers between devices  31.3 us (24%)
  waiting for transfers between devices  27.7 us (21%)
  other arithmetic  3.07 us (2%)
    pallas_call x2, Pallas kernels, finish(): pl.pallas_call(functools.partial(finish_kernel, keys), out_shape=jax.Shap...  17.5 us
    ppermute x8, starting transfers between devices, pass_on(): return part + lax.ppermute(part, 'front', [(f, f + steps[n]) for f in held])  17.1 us
    ppermute x9, waiting for transfers between devices, across(): lax.ppermute(value, 'front', [(f, f ^ bit) for f in range(front_count)])  13.2 us
    pallas_call x2, Pallas kernels, middle_step(): pl.pallas_call(functools.partial(middle_step_kernel, step), out_shape=[SQ...  13.1 us
    pallas_call x1, Pallas kernels, last_step(): pl.pallas_call(last_step_kernel, out_shape=[jax.ShapeDtypeStruct(cols.sha...  10.2 us
    pallas_call x1, Pallas kernels, assemble(): pl.pallas_call(assemble_kernel, out_shape=jax.ShapeDtypeStruct((rows, cc)...  9.89 us
    ppermute x8, waiting for transfers between devices, pass_on(): return part + lax.ppermute(part, 'front', [(f, f + steps[n]) for f in held])  9.74 us
    pallas_call x1, Pallas kernels, first_step(): pl.pallas_call(first_step_kernel, out_shape=[SQUARE] * 2, in_specs=[pl.Bl...  7.28 us
  transfers between devices with their start and end apart: 23, of which 10 were waited for; matrix products, arithmetic and copies ran while one was open for 2% of the time, Pallas kernels for 43%

commit v1 on v0

--- a/solution.py
+++ b/solution.py
@@ -254,21 +254,6 @@
     factor_step(step, u_ref, x_ref)
 
 
-def last_step_kernel(place, u_in, x_in, cols_ref, top_ref, mult_ref, u_ref, x_ref):
-    u_ref[...] = u_in[...]
-    x_ref[...] = x_in[...]
-    factor_step(S // BLK - 1, u_ref, x_ref)
-    cc = cols_ref.shape[1]
-    is_pivot = place[0] < S // cc
-    start = pl.multiple_of(jnp.minimum(place[0], S // cc - 1) * cc, cc)
-    solved = exact_dot(x_ref[...], cols_ref[...])
-    top_ref[...] = jnp.where(is_pivot, u_ref[pl.ds(start, cc), :].T, solved)
-    unit = lax.broadcasted_iota(jnp.int32, (S, cc), 0) == start + lax.broadcasted_iota(
-        jnp.int32, (S, cc), 1)
-    right = jnp.where(is_pivot, jnp.where(unit, -1.0, 0.0), solved)
-    mult_ref[...] = exact_dot(x_ref[...], right, ((0,), (0,)))
-
-
 FACTOR_PARAMS = dict(
     compiler_params=pltpu.CompilerParams(vmem_limit_bytes=48 * MIB),
     cost_estimate=pl.CostEstimate(
@@ -299,177 +284,187 @@
     )(u, x)
 
 
-def last_step(place, u, x, cols):
+def part_rows(place, part, cc):
+    slot, first, size = part
+    return pl.multiple_of(jnp.bitwise_xor(place[2], slot) * cc + first, size)
+
+
+def fill_part(place, part, rows_ref, piece_ref, mult_ref, top_ref):
+    cc = mult_ref.shape[1]
+    start = part_rows(place, part, cc)
+    is_top = jnp.logical_and(place[1] == 0, start < S)
+
+    @pl.when(is_top)
+    def _():
+        rows_ref[...] = top_ref[pl.ds(start, part[2]), :]
+
+    @pl.when(jnp.logical_not(is_top))
+    def _():
+        product = lax.dot_general(
+            piece_ref[...], mult_ref[...], (((1,), (0,)), ((), ())),
+            precision=lax.Precision.HIGH,
+            preferred_element_type=jnp.float32,
+        )
+        rows_ref[...] = jnp.where(place[0] < S // cc, 0.0, rows_ref[...]) - product
+
+
+def last_step_kernel(
+        early, late, place, index, u_in, x_in, cols_ref, front_hbm, child_hbm, recv_hbm, *refs):
+    pieces, refs = refs[:len(early)], refs[len(early):]
+    out_hbm, top_ref, mult_ref, u_ref, x_ref, rows_ref, own_ref, recv_ref, piece_ref = refs[:9]
+    rows_sems, own_sems, recv_sems, piece_sems, out_sems = refs[9:]
+    cc = cols_ref.shape[1]
+    parts = early + late
+
+    def rows_of(n):
+        return pl.ds(part_rows(place, parts[n], cc), parts[n][2])
+
+    def held(ref, n):
+        return ref.at[n, pl.ds(0, parts[n][2]), :]
+
+    def subs(n):
+        size = min(BLK, parts[n][2])
+        return [(j, size) for j in range(0, parts[n][2], size)]
+
+    def block_of(n, j):
+        return (part_rows(place, parts[n], cc) + j) // BLK
+
+    def child_copy(n, j, size, row, hbm, ref, sems):
+        start = pl.multiple_of(
+            index[row, block_of(n, j)] * BLK + (parts[n][1] + j) % BLK, size)
+        return pltpu.make_async_copy(
+            hbm.at[pl.ds(start, size), :], ref.at[n, pl.ds(j, size), :], sems.at[n, j // size])
+
+    def loads(n):
+        copies = [pltpu.make_async_copy(
+            front_hbm.at[rows_of(n), :], held(rows_ref, n), rows_sems.at[n])]
+        for j, size in subs(n):
+            copies.append(child_copy(n, j, size, 0, child_hbm, own_ref, own_sems))
+            copies.append(child_copy(n, j, size, 2, recv_hbm, recv_ref, recv_sems))
+        if n < len(early):
+            copies.append(
+                pltpu.make_async_copy(pieces[n], held(piece_ref, n), piece_sems.at[n]))
+        return copies
+
+    started = [loads(n) for n in range(len(parts))]
+    for copies in started:
+        for copy in copies:
+            copy.start()
+
+    u_ref[...] = u_in[...]
+    x_ref[...] = x_in[...]
+    factor_step(S // BLK - 1, u_ref, x_ref)
+    is_pivot = place[0] < S // cc
+    start = pl.multiple_of(jnp.minimum(place[0], S // cc - 1) * cc, cc)
+    solved = exact_dot(x_ref[...], cols_ref[...])
+    top_ref[...] = jnp.where(is_pivot, u_ref[pl.ds(start, cc), :].T, solved)
+    unit = lax.broadcasted_iota(jnp.int32, (S, cc), 0) == start + lax.broadcasted_iota(
+        jnp.int32, (S, cc), 1)
+    right = jnp.where(is_pivot, jnp.where(unit, -1.0, 0.0), solved)
+    mult_ref[...] = exact_dot(x_ref[...], right, ((0,), (0,)))
+
+    outs = []
+    for n in list(range(len(early), len(parts))) + list(range(len(early))):
+        for copy in started[n]:
+            copy.wait()
+        for j, size in subs(n):
+            rows = pl.ds(j, size)
+            block = block_of(n, j)
+            total = rows_ref[n, rows, :]
+            total += jnp.where(index[1, block] > 0, own_ref[n, rows, :], 0.0)
+            total += jnp.where(index[3, block] > 0, recv_ref[n, rows, :], 0.0)
+            rows_ref[n, rows, :] = total
+        if n < len(early):
+            fill_part(place, parts[n], held(rows_ref, n), held(piece_ref, n), mult_ref, top_ref)
+        out = pltpu.make_async_copy(held(rows_ref, n), out_hbm.at[rows_of(n), :], out_sems.at[n])
+        out.start()
+        outs.append(out)
+    for out in outs:
+        out.wait()
+
+
+def keys_of(parts):
+    return tuple((slot, first, piece.shape[0]) for slot, first, piece in parts)
+
+
+def last_step(place, index, u, x, cols, front, child, recv, early, late):
+    rows, cc = front.shape
+    count = len(early) + len(late)
+    subs = -(-cc // BLK)
+    hbm = pl.BlockSpec(memory_space=pl.ANY)
+    smem = pl.BlockSpec(memory_space=pltpu.SMEM)
+    dma = pltpu.SemaphoreType.DMA
     return pl.pallas_call(
-        last_step_kernel,
-        out_shape=[jax.ShapeDtypeStruct(cols.shape, jnp.float32)] * 2,
-        in_specs=[pl.BlockSpec(memory_space=pltpu.SMEM)] + vmem_specs(3),
-        out_specs=vmem_specs(2),
-        scratch_shapes=[pltpu.VMEM((S, S), jnp.float32)] * 2,
-        name="factor_and_solve",
-        **FACTOR_PARAMS,
-    )(place, u, x, cols)
-
-
-GROUP = 4
-
-
-def assemble_kernel(index, front_hbm, child_hbm, out_hbm, rows_ref, own_ref, *sems):
-    front_sems, own_sems, out_sems = sems
-    count = rows_ref.shape[0]
-    size = GROUP * BLK
-
-    def front_copy(n):
-        return pltpu.make_async_copy(
-            front_hbm.at[n * size:(n + 1) * size, :], rows_ref.at[n], front_sems.at[n])
-
-    def own_copy(block):
-        start = pl.multiple_of(index[0, block] * BLK, BLK)
-        return pltpu.make_async_copy(
-            child_hbm.at[pl.ds(start, BLK), :], own_ref.at[block], own_sems.at[block])
-
-    def out_copy(n):
-        return pltpu.make_async_copy(
-            rows_ref.at[n], out_hbm.at[n * size:(n + 1) * size, :], out_sems.at[n])
-
-    for n in range(count):
-        front_copy(n).start()
-        for j in range(GROUP):
-            own_copy(n * GROUP + j).start()
-    for n in range(count):
-        front_copy(n).wait()
-        for j in range(GROUP):
-            block = n * GROUP + j
-            own_copy(block).wait()
-            rows = slice(j * BLK, (j + 1) * BLK)
-            rows_ref[n, rows, :] += jnp.where(index[1, block] > 0, own_ref[block], 0.0)
-        out_copy(n).start()
-    for n in range(count):
-        out_copy(n).wait()
-
-
-def assemble(index, front, child):
-    rows, cc = front.shape
-    blocks = rows // BLK
-    count = blocks // GROUP
-    hbm = pl.BlockSpec(memory_space=pl.ANY)
-    return pl.pallas_call(
-        assemble_kernel,
-        out_shape=jax.ShapeDtypeStruct((rows, cc), jnp.float32),
-        in_specs=[pl.BlockSpec(memory_space=pltpu.SMEM), hbm, hbm],
-        out_specs=hbm,
-        scratch_shapes=[
-            pltpu.VMEM((count, GROUP * BLK, cc), jnp.float32),
-            pltpu.VMEM((blocks, BLK, cc), jnp.float32),
-            pltpu.SemaphoreType.DMA((count,)),
-            pltpu.SemaphoreType.DMA((blocks,)),
-            pltpu.SemaphoreType.DMA((count,)),
-        ],
+        functools.partial(last_step_kernel, keys_of(early), late),
+        out_shape=[jax.ShapeDtypeStruct((rows, cc), jnp.float32)]
+        + [jax.ShapeDtypeStruct((S, cc), jnp.float32)] * 2,
+        in_specs=[smem, smem] + vmem_specs(3) + [hbm] * (3 + len(early)),
+        out_specs=[hbm] + vmem_specs(2),
+        scratch_shapes=[pltpu.VMEM((S, S), jnp.float32)] * 2
+        + [pltpu.VMEM((count, cc, cc), jnp.float32)] * 3
+        + [pltpu.VMEM((len(early), cc, S), jnp.float32)]
+        + [dma((count,)), dma((count, subs)), dma((count, subs)), dma((len(early),)),
+           dma((count,))],
         compiler_params=pltpu.CompilerParams(vmem_limit_bytes=52 * MIB),
         cost_estimate=pl.CostEstimate(
-            flops=rows, bytes_accessed=16 * rows, transcendentals=0),
-        name="assemble",
-    )(index, front, child)
-
-
-def finish_kernel(parts, place, index, base_hbm, recv_hbm, mult_ref, top_ref, *refs):
+            flops=10 ** 6, bytes_accessed=4 * S, transcendentals=0),
+        name="factor_and_finish",
+    )(place, index, u, x, cols, front, child, recv, *[piece for _, _, piece in early])
+
+
+def finish_kernel(parts, place, base_hbm, mult_ref, top_ref, *refs):
     pieces, refs = refs[:len(parts)], refs[len(parts):]
-    out_hbm, rows_ref, piece_ref, recv_ref, base_sems, piece_sems, recv_sems, out_sems = refs
+    out_hbm, rows_ref, piece_ref, base_sems, piece_sems, out_sems = refs
     cc = mult_ref.shape[1]
-    is_pivot = place[0] < S // cc
-
-    def start_of(n):
-        slot, first, _ = parts[n]
-        return pl.multiple_of(jnp.bitwise_xor(place[2], slot) * cc + first, parts[n][2])
+
+    def rows_of(n):
+        return pl.ds(part_rows(place, parts[n], cc), parts[n][2])
 
     def held(ref, n):
         return ref.at[n, pl.ds(0, parts[n][2]), :]
 
-    def rows_of(n):
-        return pl.ds(start_of(n), parts[n][2])
-
-    def base_copy(n):
-        return pltpu.make_async_copy(base_hbm.at[rows_of(n), :], held(rows_ref, n), base_sems.at[n])
-
-    def piece_copy(n):
-        return pltpu.make_async_copy(pieces[n], held(piece_ref, n), piece_sems.at[n])
-
-    def recv_copy(n, j, size):
-        block = (start_of(n) + j) // BLK
-        start = pl.multiple_of(index[2, block] * BLK + (parts[n][1] + j) % BLK, size)
-        return pltpu.make_async_copy(
-            recv_hbm.at[pl.ds(start, size), :], recv_ref.at[n, pl.ds(j, size), :],
-            recv_sems.at[n, j // size])
-
-    def out_copy(n):
-        return pltpu.make_async_copy(held(rows_ref, n), out_hbm.at[rows_of(n), :], out_sems.at[n])
-
-    def pieces_of(n):
-        size = min(BLK, parts[n][2])
-        return [(j, size) for j in range(0, parts[n][2], size)]
-
+    loads = [
+        (pltpu.make_async_copy(pieces[n], held(piece_ref, n), piece_sems.at[n]),
+         pltpu.make_async_copy(base_hbm.at[rows_of(n), :], held(rows_ref, n), base_sems.at[n]))
+        for n in range(len(parts))]
+    for pair in loads:
+        for copy in pair:
+            copy.start()
+    outs = []
     for n in range(len(parts)):
-        piece_copy(n).start()
-        base_copy(n).start()
-        for j, size in pieces_of(n):
-            recv_copy(n, j, size).start()
-    for n in range(len(parts)):
-        piece_copy(n).wait()
-        base_copy(n).wait()
-        for j, size in pieces_of(n):
-            recv_copy(n, j, size).wait()
-        is_top = jnp.logical_and(place[1] == 0, start_of(n) < S)
-
-        @pl.when(is_top)
-        def _():
-            held(rows_ref, n)[...] = top_ref[rows_of(n), :]
-
-        @pl.when(jnp.logical_not(is_top))
-        def _():
-            product = lax.dot_general(
-                held(piece_ref, n)[...], mult_ref[...], (((1,), (0,)), ((), ())),
-                precision=lax.Precision.HIGH,
-                preferred_element_type=jnp.float32,
-            )
-            for j, size in pieces_of(n):
-                there = index[3, (start_of(n) + j) // BLK] > 0
-                rows = pl.ds(j, size)
-                base = rows_ref[n, rows, :] + jnp.where(there, recv_ref[n, rows, :], 0.0)
-                rows_ref[n, rows, :] = jnp.where(is_pivot, 0.0, base) - product[j:j + size, :]
-
-        out_copy(n).start()
-    for n in range(len(parts)):
-        out_copy(n).wait()
-
-
-def finish(place, index, base, recv, parts, mult, top):
+        for copy in loads[n]:
+            copy.wait()
+        fill_part(place, parts[n], held(rows_ref, n), held(piece_ref, n), mult_ref, top_ref)
+        out = pltpu.make_async_copy(held(rows_ref, n), out_hbm.at[rows_of(n), :], out_sems.at[n])
+        out.start()
+        outs.append(out)
+    for out in outs:
+        out.wait()
+
+
+def finish(place, base, parts, mult, top):
     rows, cc = base.shape
     count = len(parts)
     total = sum(piece.shape[0] for _, _, piece in parts)
     hbm = pl.BlockSpec(memory_space=pl.ANY)
     smem = pl.BlockSpec(memory_space=pltpu.SMEM)
-    keys = tuple((slot, first, piece.shape[0]) for slot, first, piece in parts)
     return pl.pallas_call(
-        functools.partial(finish_kernel, keys),
+        functools.partial(finish_kernel, keys_of(parts)),
         out_shape=jax.ShapeDtypeStruct((rows, cc), jnp.float32),
-        in_specs=[smem, smem, hbm, hbm] + vmem_specs(2) + [hbm] * count,
+        in_specs=[smem, hbm] + vmem_specs(2) + [hbm] * count,
         out_specs=hbm,
         scratch_shapes=[
             pltpu.VMEM((count, cc, cc), jnp.float32),
             pltpu.VMEM((count, cc, S), jnp.float32),
-            pltpu.VMEM((count, cc, cc), jnp.float32),
-            pltpu.SemaphoreType.DMA((count,)),
-            pltpu.SemaphoreType.DMA((count,)),
-            pltpu.SemaphoreType.DMA((count, -(-cc // BLK))),
-            pltpu.SemaphoreType.DMA((count,)),
-        ],
-        input_output_aliases={2: 0},
+        ]
+        + [pltpu.SemaphoreType.DMA((count,))] * 3,
+        input_output_aliases={1: 0},
         compiler_params=pltpu.CompilerParams(vmem_limit_bytes=48 * MIB),
         cost_estimate=pl.CostEstimate(
-            flops=6 * total * S * cc, bytes_accessed=4 * total * (3 * cc + S),
+            flops=6 * total * S * cc, bytes_accessed=4 * total * (2 * cc + S),
             transcendentals=0),
         name="finish",
-    )(place, index, base, recv, mult, top, *[piece for _, _, piece in parts])
+    )(place, base, mult, top, *[piece for _, _, piece in parts])
 
 
 def block_places(blocks, first, count, shift, limit):
@@ -557,13 +552,12 @@
         sent = child_rows(later, child, row_count)
         parts = [pass_on(part, order, 1) for part, order in zip(parts, orders)]
         parts, sent, index = barrier((parts, sent, index))
-        base = assemble(index, front_block, child)
         for n in range(2, len(orders[0]) - 1):
             parts = [pass_on(part, order, n) for part, order in zip(parts, orders)]
-        parts, came, base = barrier((parts, came, base))
+        parts, came, sent = barrier((parts, came, sent))
+        recv = lax.ppermute(sent, "leaf", swap)
     else:
-        sent = child_rows(leaf_index, child, row_count)
-        base = assemble(index, front_block, child)
+        recv = lax.ppermute(child_rows(leaf_index, child, row_count), "leaf", swap)
         sources = [spread_pivot(cols, front_index, front_count, S // col_count)]
     piece = jnp.where(own, piece, came)
 
@@ -578,17 +572,16 @@
         parts, held = barrier((parts, held))
         sources = parts + [lax.ppermute(part, "leaf", swap) for part in parts]
     over = [across(part, 4) for part in held]
-    sources, sides = barrier((sources, sides))
     cut = col_count // 2
+    u, x = first_step(place, sources)
+    u, x, sides = barrier((u, x, sides))
     crossed = [(across(xs[:cut], 2), across(ys[cut:], 1)) for xs, ys in sides]
-    u, x = first_step(place, sources)
     u, x = middle_step(1, u, x)
-    u, x, over, crossed, sent = barrier((u, x, over, crossed, sent))
-    recv = lax.ppermute(sent, "leaf", swap)
+    u, x, over = barrier((u, x, over))
     over_sides = [(across(part, 1), across(part, 2)) for part in over]
+    u, x = middle_step(2, u, x)
+    u, x, crossed = barrier((u, x, crossed))
     over_crossed = [(across(low, 4), across(high, 4)) for low, high in crossed]
-    u, x = middle_step(2, u, x)
-    top, mult = last_step(place, u, x, cols)
 
     early, late = [], []
     for group, first, alone, beside, cross in (
@@ -598,9 +591,9 @@
             early.append((slot, 0, part))
             group += [(slot + 1, 0, xs), (slot + 2, 0, ys)]
             group += [(slot + 3, 0, low), (slot + 3, cut, high)]
-    for group in (early, late):
-        base = finish(place, index, base, recv, group, mult, top)
-    return base
+    base, top, mult = last_step(
+        place, index, u, x, cols, front_block, child, recv, early, keys_of(late))
+    return finish(place, base, late, mult, top)
 
 
 def solution(mesh):

time: 133 us -> 132 us (level)
  Pallas kernels: 68.8 us -> 61.2 us
  local copies, waits for them, and re-layouts: 1.31 us -> 6.76 us
  starting transfers between devices: 31.3 us -> 35.1 us
  other arithmetic: 3.07 us -> 1.22 us
  waiting for transfers between devices: 27.7 us -> 26 us
    ppermute x9, waiting for transfers between devices: 13.2 us -> 4.64 us  [across(): lax.ppermute(value, 'front', [(f, f ^ bit) for f in range(front_count)])]
    pallas_call x4 -> x2, Pallas kernels: 37.6 us -> 30.1 us  [the longest x1 24 us: last_step(): pl.pallas_call(functools.partial(last_step_kernel, keys_of(early), late),...]
    ppermute x9, starting transfers between devices: 7.07 us -> 12.8 us  [across(): lax.ppermute(value, 'front', [(f, f ^ bit) for f in range(front_count)])]
    unnamed x10 -> x24, local copies, waits for them, and re-layouts: 1.24 us -> 6.69 us
    ppermute x8, waiting for transfers between devices: 9.74 us -> 15.1 us  [pass_on(): return part + lax.ppermute(part, 'front', [(f, f + steps[n]) for f in held])]
    add x8, other arithmetic: 2 us -> 0.16 us  [pass_on(): return part + lax.ppermute(part, 'front', [(f, f + steps[n]) for f in held])]
    ppermute x2, waiting for transfers between devices: 1.12 us -> 2.64 us  [per_device(): sources = parts + [lax.ppermute(part, 'leaf', swap) for part in parts]]
    ppermute x8, starting transfers between devices: 17.1 us -> 15.6 us  [pass_on(): return part + lax.ppermute(part, 'front', [(f, f + steps[n]) for f in held])]
  transfers between devices with their start and end apart: 23 -> 23, of which waited for: 10 -> 13; matrix products, arithmetic and copies ran while one was open for 2% -> 1% of each run, Pallas kernels for 43% -> 39%
where the time goes in v1:
time: 132 us; the launch traced here: 131 us
  Pallas kernels  61.2 us (46%)
  starting transfers between devices  35.1 us (27%)
  waiting for transfers between devices  26 us (20%)
  local copies, waits for them, and re-layouts  6.76 us (5%)
    pallas_call x1, Pallas kernels, last_step(): pl.pallas_call(functools.partial(last_step_kernel, keys_of(early), late),...  24 us
    ppermute x8, starting transfers between devices, pass_on(): return part + lax.ppermute(part, 'front', [(f, f + steps[n]) for f in held])  15.6 us
    ppermute x8, waiting for transfers between devices, pass_on(): return part + lax.ppermute(part, 'front', [(f, f + steps[n]) for f in held])  15.1 us
    pallas_call x2, Pallas kernels, middle_step(): pl.pallas_call(functools.partial(middle_step_kernel, step), out_shape=[SQ...  13.1 us
    ppermute x9, starting transfers between devices, across(): lax.ppermute(value, 'front', [(f, f ^ bit) for f in range(front_count)])  12.8 us
    pallas_call x1, Pallas kernels, first_step(): pl.pallas_call(first_step_kernel, out_shape=[SQUARE] * 2, in_specs=[pl.Bl...  7.29 us
    unnamed x24, local copies, waits for them, and re-layouts  6.69 us
    pallas_call x1, Pallas kernels, child_rows(): pl.pallas_call(functools.partial(child_rows_kernel, pieces), out_shape=ja...  6.43 us
  transfers between devices with their start and end apart: 23, of which 13 were waited for; matrix products, arithmetic and copies ran while one was open for 1% of the time, Pallas kernels for 39%

profile of v1, /device:TPU:0, one launch (start us, length us, event | category | flops | bytes accessed | tf_op | source)
XLA Modules:
  0.0 130.9 jit_solution(15799567500508050734)
XLA Ops:
  0.6 3.4 %pivot_rows.1.mine_ref = f32[512,512]{1,0:T(8,128)} custom-call(s32[3]{0:T(128)} %pad_add_fusion.1.place, s32[48]{0:T(128)} %bitcast.15, f32[4096,512]{1,0:T(8,128)} %front_hbm.3, f32[6144,512]{1,0:T(8,128)} %bitcast.12), custom_call_target="tpu_custom_call" | custom-call | flops 1048576 | bytes 3145728 | tf_op jit(solution)/shard_map/pivot_rows/pallas_call | solution.py:113
  4.5 2.5 %collective-permute-done.other_ref = f32[512,512]{1,0:T(8,128)S(1)} collective-permute-done((f32[512,512]{1,0:T(8,128)}, f32[512,512]{1,0:T(8,128)S(1)}, u32[]{:S(2)}, u32[]{:S(2)}) %collective-permute-start) | collective-permute-done | bytes 1048608 | tf_op jit(solution)/shard_map/ppermute | solution.py:526
  10.2 5.9 %collective-permute-start.8 = (f32[512,512]{1,0:T(8,128)S(1)}, f32[512,512]{1,0:T(8,128)S(1)}, u32[]{:S(2)}, u32[]{:S(2)}) collective-permute-start(f32[512,512]{1,0:T(8,128)S(1)} %get-tuple-element.51), channel_id=1, source_target_pairs={{0,8},{1,9},{2,10},{3,11},{4,12},{5,13},{6,14},{7,15},{24,16},{25,... | collective-permute-start | bytes 3145736 | tf_op jit(solution)/shard_map/ppermute | solution.py:530
  17.6 3.4 %collective-permute-start.2 = (f32[320,128]{1,0:T(8,128)S(1)}, f32[320,128]{1,0:T(8,128)S(1)}, u32[]{:S(2)}, u32[]{:S(2)}) collective-permute-start(f32[320,128]{1,0:T(8,128)S(1)} %get-tuple-element.44), channel_id=1, source_target_pairs={{0,2},{16,18}} | collective-permute-start | bytes 491528 | tf_op jit(solution)/shard_map/ppermute | solution.py:509
  21.0 1.3 collective-permute-start.1
  22.3 2.5 %collective-permute-done.2 = f32[320,128]{1,0:T(8,128)S(1)} collective-permute-done((f32[320,128]{1,0:T(8,128)S(1)}, f32[320,128]{1,0:T(8,128)S(1)}, u32[]{:S(2)}, u32[]{:S(2)}) %collective-permute-start.2) | collective-permute-done | bytes 163872 | tf_op jit(solution)/shard_map/ppermute | solution.py:509
  26.1 4.4 %collective-permute-start.4 = (f32[320,128]{1,0:T(8,128)S(1)}, f32[320,128]{1,0:T(8,128)S(1)}, u32[]{:S(2)}, u32[]{:S(2)}) collective-permute-start(f32[320,128]{1,0:T(8,128)S(1)} %add.60), channel_id=1, source_target_pairs={{0,1},{2,3},{16,17},{18,19}} | collective-permute-start | bytes 491528 | tf_op jit(solution)/shard_map/ppermute | solution.py:509
  30.5 1.3 collective-permute-start.3
  31.9 6.4 %child_rows.1 = f32[4096,512]{1,0:T(8,128)} custom-call(s32[1]{0:T(128)} %bitcast.5.leaf, f32[6144,512]{1,0:T(8,128)} %bitcast.13), custom_call_target="tpu_custom_call" | custom-call | bytes 2048 | tf_op jit(solution)/shard_map/child_rows/pallas_call | solution.py:153
  38.4 1.3 collective-permute-start.7
  41.0 3.3 %collective-permute-done.7 = f32[320,128]{1,0:T(8,128)S(1)} collective-permute-done((f32[320,128]{1,0:T(8,128)S(1)}, f32[320,128]{1,0:T(8,128)S(1)}, u32[]{:S(2)}, u32[]{:S(2)}) %collective-permute-start.7) | collective-permute-done | bytes 163872 | tf_op jit(solution)/shard_map/ppermute | solution.py:509
  44.3 1.8 %collective-permute-done.6 = f32[320,128]{1,0:T(8,128)S(1)} collective-permute-done((f32[320,128]{1,0:T(8,128)S(1)}, f32[320,128]{1,0:T(8,128)S(1)}, u32[]{:S(2)}, u32[]{:S(2)}) %collective-permute-start.6) | collective-permute-done | bytes 163872 | tf_op jit(solution)/shard_map/ppermute | solution.py:509
  49.3 2.9 %collective-permute-done.10 = f32[320,128]{1,0:T(8,128)S(1)} collective-permute-done((f32[320,128]{1,0:T(8,128)S(1)}, f32[320,128]{1,0:T(8,128)S(1)}, u32[]{:S(2)}, u32[]{:S(2)}) %collective-permute-start.10) | collective-permute-done | bytes 163872 | tf_op jit(solution)/shard_map/ppermute | solution.py:509
  52.2 3.3 %collective-permute-done.9 = f32[320,128]{1,0:T(8,128)S(1)} collective-permute-done((f32[320,128]{1,0:T(8,128)S(1)}, f32[320,128]{1,0:T(8,128)S(1)}, u32[]{:S(2)}, u32[]{:S(2)}) %collective-permute-start.9) | collective-permute-done | bytes 163872 | tf_op jit(solution)/shard_map/ppermute | solution.py:509
  55.5 8.5 %collective-permute-start.15 = (f32[512,512]{1,0:T(8,128)S(1)}, f32[512,512]{1,0:T(8,128)S(1)}, u32[]{:S(2)}, u32[]{:S(2)}) collective-permute-start(f32[512,512]{1,0:T(8,128)S(1)} %broadcast_select_fusion.refs_0_), channel_id=1, source_target_pairs={{0,4},{1,5},{2,6},{3,7},{4,0},{5,1},{6,2},{7,3},{8,12},{9,13},{10,... | collective-permute-start | bytes 3145736 | tf_op jit(solution)/shard_map/ppermute | solution.py:540
  64.1 1.4 %collective-permute-done.11.refs_2_ = f32[320,128]{1,0:T(8,128)S(1)} collective-permute-done((f32[320,128]{1,0:T(8,128)S(1)}, f32[320,128]{1,0:T(8,128)S(1)}, u32[]{:S(2)}, u32[]{:S(2)}) %collective-permute-start.11) | collective-permute-done | bytes 163872 | tf_op jit(solution)/shard_map/ppermute | solution.py:573
  66.8 7.3 %factor_step.3 = (f32[512,512]{1,0:T(8,128)S(1)}, f32[512,512]{1,0:T(8,128)S(1)}) custom-call(s32[3]{0:T(128)S(1)} %copy-done.6, f32[320,128]{1,0:T(8,128)S(1)} %add.67.refs_0_, f32[320,128]{1,0:T(8,128)S(1)} %add.68.refs_1_, f32[320,128]{1,0:T(8,128)S(1)} %collective-permute-done.11.refs_2_, f32[320,128]{1,0:T(8,128)S(1)} %collective-permute-done.12.refs_3_), custom_call_target="tpu_custom_call" | custom-call | flops 1000000 | bytes 2048 | tf_op jit(solution)/shard_map/factor_step/pallas_call | solution.py:266
  75.3 1.7 %collective-permute-start.17 = (f32[256,512]{1,0:T(8,128)S(1)}, f32[256,512]{1,0:T(8,128)S(1)}, u32[]{:S(2)}, u32[]{:S(2)}) collective-permute-start(f32[256,512]{1,0:T(8,128)S(1)} %slice.7), channel_id=1, source_target_pairs={{0,1},{1,0},{2,3},{3,2},{4,5},{5,4},{6,7},{7,6},{8,9},{9,8},{10,11... | collective-permute-start | bytes 1572872 | tf_op jit(solution)/shard_map/ppermute | solution.py:540
  77.0 6.5 %factor_step.4 = (f32[512,512]{1,0:T(8,128)S(1)}, f32[512,512]{1,0:T(8,128)S(1)}) custom-call(f32[512,512]{1,0:T(8,128)S(1)} %get-tuple-element.60.u_in, f32[512,512]{1,0:T(8,128)S(1)} %get-tuple-element.61.x_in), custom_call_target="tpu_custom_call" | custom-call | flops 1000000 | bytes 2048 | tf_op jit(solution)/shard_map/factor_step/pallas_call | solution.py:277
  83.5 3.9 %collective-permute-done.15.refs_5_ = f32[512,512]{1,0:T(8,128)S(1)} collective-permute-done((f32[512,512]{1,0:T(8,128)S(1)}, f32[512,512]{1,0:T(8,128)S(1)}, u32[]{:S(2)}, u32[]{:S(2)}) %collective-permute-start.15) | collective-permute-done | bytes 1048608 | tf_op jit(solution)/shard_map/ppermute | solution.py:540
  87.5 6.5 %factor_step.5 = (f32[512,512]{1,0:T(8,128)S(1)}, f32[512,512]{1,0:T(8,128)S(1)}) custom-call(f32[512,512]{1,0:T(8,128)S(1)} %get-tuple-element.65.u_in, f32[512,512]{1,0:T(8,128)S(1)} %get-tuple-element.66.x_in), custom_call_target="tpu_custom_call" | custom-call | flops 1000000 | bytes 2048 | tf_op jit(solution)/shard_map/factor_step/pallas_call | solution.py:277
  96.0 1.7 %collective-permute-start.21 = (f32[256,512]{1,0:T(8,128)S(1)}, f32[256,512]{1,0:T(8,128)S(1)}, u32[]{:S(2)}, u32[]{:S(2)}) collective-permute-start(f32[256,512]{1,0:T(8,128)S(1)} %collective-permute-done.16.refs_3_), channel_id=1, source_target_pairs={{0,4},{1,5},{2,6},{3,7},{4,0},{5,1},{6,2},{7,3},{8,12},{9,13},{10,... | collective-permute-start | bytes 1572872 | tf_op jit(solution)/shard_map/ppermute | solution.py:540
  98.1 24.0 %factor_and_finish.1 = (f32[4096,512]{1,0:T(8,128)}, f32[512,512]{1,0:T(8,128)}, f32[512,512]{1,0:T(8,128)}) custom-call(s32[3]{0:T(128)S(1)} %copy-done.6, s32[4,32]{1,0:T(4,128)S(1)} %pad_add_fusion.index, f32[512,512]{1,0:T(8,128)} %copy-done.2, f32[512,512]{1,0:T(8,128)} %copy-done.3, f32[512,512]{1,0:T(8,128)} %copy-done.1, f32[4096,512]{1,0:T(8,128)} %front_hbm.3, ...), custom_call_target="tpu_custom_call" | custom-call | flops 1000000 | bytes 2048 | tf_op jit(solution)/shard_map/factor_and_finish/pallas_call | solution.py:397
  124.6 6.1 %finish.1 = f32[4096,512]{1,0:T(8,128)} custom-call(s32[3]{0:T(128)S(1)} %copy-done.6, f32[4096,512]{1,0:T(8,128)} %get-tuple-element.78.base_hbm, f32[512,512]{1,0:T(8,128)S(1)} %copy-done.5, f32[512,512]{1,0:T(8,128)S(1)} %copy-done.4, f32[512,512]{1,0:T(8,128)S(1)} %collective-permute-done.19.refs_0_, ...), custom_call_target="tpu_custom_call", output_to_operand_aliasing={{}: (1, {})} | custom-call | flops 2415919104 | bytes 9437184 | tf_op jit(solution)/shard_map/finish/pallas_call | solution.py:451
  (71 shorter events, 18.7 us)
Async XLA Ops:
  4.0 3.0 %collective-permute-start = (f32[512,512]{1,0:T(8,128)}, f32[512,512]{1,0:T(8,128)S(1)}, u32[]{:S(2)}, u32[]{:S(2)}) collective-permute-start(f32[512,512]{1,0:T(8,128)} %pivot_rows.1.mine_ref), channel_id=1, source_target_pairs={{0,16},{16,0},{1,17},{17,1},{2,18},{18,2},{3,19},{19,3},{4,20},{20... | collective-permute-start | bytes 3145736 | tf_op jit(solution)/shard_map/ppermute | solution.py:526
  10.2 36.0 %collective-permute-start.8 = (f32[512,512]{1,0:T(8,128)S(1)}, f32[512,512]{1,0:T(8,128)S(1)}, u32[]{:S(2)}, u32[]{:S(2)}) collective-permute-start(f32[512,512]{1,0:T(8,128)S(1)} %get-tuple-element.51), channel_id=1, source_target_pairs={{0,8},{1,9},{2,10},{3,11},{4,12},{5,13},{6,14},{7,15},{24,16},{25,... | collective-permute-start | bytes 3145736 | tf_op jit(solution)/shard_map/ppermute | solution.py:530
  16.2 1.2 collective-permute-start.5
  17.6 7.2 %collective-permute-start.2 = (f32[320,128]{1,0:T(8,128)S(1)}, f32[320,128]{1,0:T(8,128)S(1)}, u32[]{:S(2)}, u32[]{:S(2)}) collective-permute-start(f32[320,128]{1,0:T(8,128)S(1)} %get-tuple-element.44), channel_id=1, source_target_pairs={{0,2},{16,18}} | collective-permute-start | bytes 491528 | tf_op jit(solution)/shard_map/ppermute | solution.py:509
  21.0 5.1 %collective-permute-start.1 = (f32[320,128]{1,0:T(8,128)S(1)}, f32[320,128]{1,0:T(8,128)S(1)}, u32[]{:S(2)}, u32[]{:S(2)}) collective-permute-start(f32[320,128]{1,0:T(8,128)S(1)} %get-tuple-element.43), channel_id=1, source_target_pairs={{0,1},{16,17}} | collective-permute-start | bytes 491528 | tf_op jit(solution)/shard_map/ppermute | solution.py:509
  26.1 12.2 %collective-permute-start.4 = (f32[320,128]{1,0:T(8,128)S(1)}, f32[320,128]{1,0:T(8,128)S(1)}, u32[]{:S(2)}, u32[]{:S(2)}) collective-permute-start(f32[320,128]{1,0:T(8,128)S(1)} %add.60), channel_id=1, source_target_pairs={{0,1},{2,3},{16,17},{18,19}} | collective-permute-start | bytes 491528 | tf_op jit(solution)/shard_map/ppermute | solution.py:509
  30.5 7.8 %collective-permute-start.3 = (f32[320,128]{1,0:T(8,128)S(1)}, f32[320,128]{1,0:T(8,128)S(1)}, u32[]{:S(2)}, u32[]{:S(2)}) collective-permute-start(f32[320,128]{1,0:T(8,128)S(1)} %add.59), channel_id=1, source_target_pairs={{0,2},{1,3},{16,18},{17,19}} | collective-permute-start | bytes 491528 | tf_op jit(solution)/shard_map/ppermute | solution.py:509
  38.4 5.9 %collective-permute-start.7 = (f32[320,128]{1,0:T(8,128)S(1)}, f32[320,128]{1,0:T(8,128)S(1)}, u32[]{:S(2)}, u32[]{:S(2)}) collective-permute-start(f32[320,128]{1,0:T(8,128)S(1)} %add.62), channel_id=1, source_target_pairs={{0,4},{2,6},{1,5},{3,7},{16,20},{18,22},{17,21},{19,23}} | collective-permute-start | bytes 491528 | tf_op jit(solution)/shard_map/ppermute | solution.py:509
  39.7 6.5 %collective-permute-start.6 = (f32[320,128]{1,0:T(8,128)S(1)}, f32[320,128]{1,0:T(8,128)S(1)}, u32[]{:S(2)}, u32[]{:S(2)}) collective-permute-start(f32[320,128]{1,0:T(8,128)S(1)} %add.61), channel_id=1, source_target_pairs={{0,4},{1,5},{2,6},{3,7},{16,20},{17,21},{18,22},{19,23}} | collective-permute-start | bytes 491528 | tf_op jit(solution)/shard_map/ppermute | solution.py:509
  46.2 51.8 %collective-permute-start.18 = (f32[4096,512]{1,0:T(8,128)}, f32[4096,512]{1,0:T(8,128)}, u32[]{:S(2)}, u32[]{:S(2)}) collective-permute-start(f32[4096,512]{1,0:T(8,128)} %child_rows.1), channel_id=1, source_target_pairs={{0,16},{16,0},{1,17},{17,1},{2,18},{18,2},{3,19},{19,3},{4,20},{20... | collective-permute-start | bytes 25165832 | tf_op jit(solution)/shard_map/ppermute | solution.py:558
  46.3 5.9 %collective-permute-start.10 = (f32[320,128]{1,0:T(8,128)S(1)}, f32[320,128]{1,0:T(8,128)S(1)}, u32[]{:S(2)}, u32[]{:S(2)}) collective-permute-start(f32[320,128]{1,0:T(8,128)S(1)} %add.66), channel_id=1, source_target_pairs={{0,8},{2,10},{1,9},{3,11},{4,12},{6,14},{5,13},{7,15},{16,24},{18,... | collective-permute-start | bytes 491528 | tf_op jit(solution)/shard_map/ppermute | solution.py:509
  47.6 7.9 %collective-permute-start.9 = (f32[320,128]{1,0:T(8,128)S(1)}, f32[320,128]{1,0:T(8,128)S(1)}, u32[]{:S(2)}, u32[]{:S(2)}) collective-permute-start(f32[320,128]{1,0:T(8,128)S(1)} %add.65), channel_id=1, source_target_pairs={{0,8},{1,9},{2,10},{3,11},{4,12},{5,13},{6,14},{7,15},{16,24},{17,... | collective-permute-start | bytes 491528 | tf_op jit(solution)/shard_map/ppermute | solution.py:509
  49.1 48.9 %copy-start.7 = (f32[512,512]{1,0:T(8,128)}, f32[512,512]{1,0:T(8,128)S(1)}, u32[]{:S(2)}) copy-start(f32[512,512]{1,0:T(8,128)S(1)} %broadcast_select_fusion.refs_0_) | copy-start | bytes 3145732
  49.1 25.6 %collective-permute-start.13 = (f32[512,512]{1,0:T(8,128)S(1)}, f32[512,512]{1,0:T(8,128)S(1)}, u32[]{:S(2)}, u32[]{:S(2)}) collective-permute-start(f32[512,512]{1,0:T(8,128)S(1)} %broadcast_select_fusion.refs_0_), channel_id=1, source_target_pairs={{0,1},{1,0},{2,3},{3,2},{4,5},{5,4},{6,7},{7,6},{8,9},{9,8},{10,11... | collective-permute-start | bytes 3145736 | tf_op jit(solution)/shard_map/ppermute | solution.py:540
  49.2 25.6 %collective-permute-start.14 = (f32[512,512]{1,0:T(8,128)S(1)}, f32[512,512]{1,0:T(8,128)S(1)}, u32[]{:S(2)}, u32[]{:S(2)}) collective-permute-start(f32[512,512]{1,0:T(8,128)S(1)} %broadcast_select_fusion.refs_0_), channel_id=1, source_target_pairs={{0,2},{1,3},{2,0},{3,1},{4,6},{5,7},{6,4},{7,5},{8,10},{9,11},{10,... | collective-permute-start | bytes 3145736 | tf_op jit(solution)/shard_map/ppermute | solution.py:540
  55.5 31.9 %collective-permute-start.15 = (f32[512,512]{1,0:T(8,128)S(1)}, f32[512,512]{1,0:T(8,128)S(1)}, u32[]{:S(2)}, u32[]{:S(2)}) collective-permute-start(f32[512,512]{1,0:T(8,128)S(1)} %broadcast_select_fusion.refs_0_), channel_id=1, source_target_pairs={{0,4},{1,5},{2,6},{3,7},{4,0},{5,1},{6,2},{7,3},{8,12},{9,13},{10,... | collective-permute-start | bytes 3145736 | tf_op jit(solution)/shard_map/ppermute | solution.py:540
  64.1 1.4 %collective-permute-start.11 = (f32[320,128]{1,0:T(8,128)S(1)}, f32[320,128]{1,0:T(8,128)S(1)}, u32[]{:S(2)}, u32[]{:S(2)}) collective-permute-start(f32[320,128]{1,0:T(8,128)S(1)} %add.67.refs_0_), channel_id=1, source_target_pairs={{0,16},{16,0},{1,17},{17,1},{2,18},{18,2},{3,19},{19,3},{4,20},{20... | collective-permute-start | bytes 491528 | tf_op jit(solution)/shard_map/ppermute | solution.py:573
  65.4 1.4 %collective-permute-start.12 = (f32[320,128]{1,0:T(8,128)S(1)}, f32[320,128]{1,0:T(8,128)S(1)}, u32[]{:S(2)}, u32[]{:S(2)}) collective-permute-start(f32[320,128]{1,0:T(8,128)S(1)} %add.68.refs_1_), channel_id=1, source_target_pairs={{0,16},{16,0},{1,17},{17,1},{2,18},{18,2},{3,19},{19,3},{4,20},{20... | collective-permute-start | bytes 491528 | tf_op jit(solution)/shard_map/ppermute | solution.py:573
  74.9 21.1 %collective-permute-start.16 = (f32[256,512]{1,0:T(8,128)S(1)}, f32[256,512]{1,0:T(8,128)S(1)}, u32[]{:S(2)}, u32[]{:S(2)}) collective-permute-start(f32[256,512]{1,0:T(8,128)S(1)} %slice.6), channel_id=1, source_target_pairs={{0,2},{1,3},{2,0},{3,1},{4,6},{5,7},{6,4},{7,5},{8,10},{9,11},{10,... | collective-permute-start | bytes 1572872 | tf_op jit(solution)/shard_map/ppermute | solution.py:540
  75.3 20.7 %collective-permute-start.17 = (f32[256,512]{1,0:T(8,128)S(1)}, f32[256,512]{1,0:T(8,128)S(1)}, u32[]{:S(2)}, u32[]{:S(2)}) collective-permute-start(f32[256,512]{1,0:T(8,128)S(1)} %slice.7), channel_id=1, source_target_pairs={{0,1},{1,0},{2,3},{3,2},{4,5},{5,4},{6,7},{7,6},{8,9},{9,8},{10,11... | collective-permute-start | bytes 1572872 | tf_op jit(solution)/shard_map/ppermute | solution.py:540
  87.5 34.7 %collective-permute-start.19 = (f32[512,512]{1,0:T(8,128)S(1)}, f32[512,512]{1,0:T(8,128)S(1)}, u32[]{:S(2)}, u32[]{:S(2)}) collective-permute-start(f32[512,512]{1,0:T(8,128)S(1)} %collective-permute-done.15.refs_5_), channel_id=1, source_target_pairs={{0,1},{1,0},{2,3},{3,2},{4,5},{5,4},{6,7},{7,6},{8,9},{9,8},{10,11... | collective-permute-start | bytes 3145736 | tf_op jit(solution)/shard_map/ppermute | solution.py:540
  87.5 34.7 %collective-permute-start.20 = (f32[512,512]{1,0:T(8,128)S(1)}, f32[512,512]{1,0:T(8,128)S(1)}, u32[]{:S(2)}, u32[]{:S(2)}) collective-permute-start(f32[512,512]{1,0:T(8,128)S(1)} %collective-permute-done.15.refs_5_), channel_id=1, source_target_pairs={{0,2},{1,3},{2,0},{3,1},{4,6},{5,7},{6,4},{7,5},{8,10},{9,11},{10,... | collective-permute-start | bytes 3145736 | tf_op jit(solution)/shard_map/ppermute | solution.py:540
  96.0 26.1 %collective-permute-start.21 = (f32[256,512]{1,0:T(8,128)S(1)}, f32[256,512]{1,0:T(8,128)S(1)}, u32[]{:S(2)}, u32[]{:S(2)}) collective-permute-start(f32[256,512]{1,0:T(8,128)S(1)} %collective-permute-done.16.refs_3_), channel_id=1, source_target_pairs={{0,4},{1,5},{2,6},{3,7},{4,0},{5,1},{6,2},{7,3},{8,12},{9,13},{10,... | collective-permute-start | bytes 1572872 | tf_op jit(solution)/shard_map/ppermute | solution.py:540
  97.7 24.4 %collective-permute-start.22 = (f32[256,512]{1,0:T(8,128)S(1)}, f32[256,512]{1,0:T(8,128)S(1)}, u32[]{:S(2)}, u32[]{:S(2)}) collective-permute-start(f32[256,512]{1,0:T(8,128)S(1)} %collective-permute-done.17.refs_4_), channel_id=1, source_target_pairs={{0,4},{1,5},{2,6},{3,7},{4,0},{5,1},{6,2},{7,3},{8,12},{9,13},{10,... | collective-permute-start | bytes 1572872 | tf_op jit(solution)/shard_map/ppermute | solution.py:540
  (11 other events, 85.7 us)

commit v2 on v1

--- a/solution.py
+++ b/solution.py
@@ -124,45 +124,6 @@
     )(place, blocks, front, child)
 
 
-def child_rows_kernel(pieces, leaf, child_hbm, out_hbm, rows_ref, in_sems, out_sems):
-    rows = out_hbm.shape[0]
-    size = rows // pieces
-    first = (1 - leaf[0]) * (child_hbm.shape[0] - rows)
-
-    def in_copy(n):
-        start = pl.multiple_of(first + n * size, BLK)
-        return pltpu.make_async_copy(
-            child_hbm.at[pl.ds(start, size), :], rows_ref.at[n], in_sems.at[n])
-
-    def out_copy(n):
-        return pltpu.make_async_copy(
-            rows_ref.at[n], out_hbm.at[n * size:(n + 1) * size, :], out_sems.at[n])
-
-    for n in range(pieces):
-        in_copy(n).start()
-    for n in range(pieces):
-        in_copy(n).wait()
-        out_copy(n).start()
-    for n in range(pieces):
-        out_copy(n).wait()
-
-
-def child_rows(leaf, child, rows):
-    pieces = 8
-    hbm = pl.BlockSpec(memory_space=pl.ANY)
-    return pl.pallas_call(
-        functools.partial(child_rows_kernel, pieces),
-        out_shape=jax.ShapeDtypeStruct((rows, child.shape[1]), jnp.float32),
-        in_specs=[pl.BlockSpec(memory_space=pltpu.SMEM), hbm],
-        out_specs=hbm,
-        scratch_shapes=[pltpu.VMEM((pieces, rows // pieces, child.shape[1]), jnp.float32)]
-        + [pltpu.SemaphoreType.DMA((pieces,))] * 2,
-        compiler_params=pltpu.CompilerParams(vmem_limit_bytes=56 * MIB),
-        cost_estimate=pl.CostEstimate(flops=0, bytes_accessed=4 * S, transcendentals=0),
-        name="child_rows",
-    )(leaf.reshape(1), child)
-
-
 def packed_blocks():
     count = S // BLK
     order = [(i, j) for i in range(count) for j in range(i, count)]
@@ -208,10 +169,11 @@
     )(place, mine, other)
 
 
-def factor_step(step, u_ref, x_ref):
+def factor_step(step, u_ref, x_ref, between=lambda: None):
     rows = slice(step * BLK, (step + 1) * BLK)
     done, rest = slice(0, (step + 1) * BLK), slice((step + 1) * BLK, S)
     block, inverse, pivots = eliminate_block(u_ref[rows, rows])
+    between()
     scale = lax.rsqrt(pivots)
     scale = scale * (1.5 - 0.5 * pivots * scale * scale)
     r = lax.broadcasted_iota(jnp.int32, (BLK, BLK), 0)
@@ -229,9 +191,28 @@
         x_ref[rest, done] -= exact_dot(u, x, ((0,), (0,)))
 
 
-def first_step_kernel(place, *refs):
-    u_ref, x_ref = refs[-2:]
-    sources = refs[:-2]
+def first_step_kernel(place, child_hbm, *refs):
+    sources = refs[:-6]
+    u_ref, x_ref, sent_hbm, rows_ref, in_sems, out_sems = refs[-6:]
+    count, size = rows_ref.shape[:2]
+    first = (1 - place[1]) * (child_hbm.shape[0] - count * size)
+    ins = [
+        pltpu.make_async_copy(
+            child_hbm.at[pl.ds(pl.multiple_of(first + n * size, BLK), size), :],
+            rows_ref.at[n], in_sems.at[n])
+        for n in range(count)]
+    outs = [
+        pltpu.make_async_copy(
+            rows_ref.at[n], sent_hbm.at[n * size:(n + 1) * size, :], out_sems.at[n])
+        for n in range(count)]
+    for copy in ins:
+        copy.start()
+
+    def between():
+        for copy_in, copy_out in zip(ins, outs):
+            copy_in.wait()
+            copy_out.start()
+
     if len(sources) == 1:
         u_ref[...] = sources[0][...]
     else:
@@ -245,7 +226,9 @@
     eye = lax.broadcasted_iota(jnp.int32, (S, S), 0) == lax.broadcasted_iota(
         jnp.int32, (S, S), 1)
     x_ref[...] = jnp.where(eye, 1.0, 0.0)
-    factor_step(0, u_ref, x_ref)
+    factor_step(0, u_ref, x_ref, between)
+    for copy in outs:
+        copy.wait()
 
 
 def middle_step_kernel(step, u_in, x_in, u_ref, x_ref):
@@ -262,15 +245,20 @@
 SQUARE = jax.ShapeDtypeStruct((S, S), jnp.float32)
 
 
-def first_step(place, sources):
+def first_step(place, sources, child, rows):
+    pieces = 8
+    cc = child.shape[1]
+    hbm = pl.BlockSpec(memory_space=pl.ANY)
     return pl.pallas_call(
         first_step_kernel,
-        out_shape=[SQUARE] * 2,
-        in_specs=[pl.BlockSpec(memory_space=pltpu.SMEM)] + vmem_specs(len(sources)),
-        out_specs=vmem_specs(2),
+        out_shape=[SQUARE] * 2 + [jax.ShapeDtypeStruct((rows, cc), jnp.float32)],
+        in_specs=[pl.BlockSpec(memory_space=pltpu.SMEM), hbm] + vmem_specs(len(sources)),
+        out_specs=vmem_specs(2) + [hbm],
+        scratch_shapes=[pltpu.VMEM((pieces, rows // pieces, cc), jnp.float32)]
+        + [pltpu.SemaphoreType.DMA((pieces,))] * 2,
         name="factor_step",
         **FACTOR_PARAMS,
-    )(place, *sources)
+    )(place, child, *sources)
 
 
 def middle_step(step, u, x):
@@ -405,7 +393,7 @@
         + [pltpu.VMEM((len(early), cc, S), jnp.float32)]
         + [dma((count,)), dma((count, subs)), dma((count, subs)), dma((len(early),)),
            dma((count,))],
-        compiler_params=pltpu.CompilerParams(vmem_limit_bytes=52 * MIB),
+        compiler_params=pltpu.CompilerParams(vmem_limit_bytes=48 * MIB),
         cost_estimate=pl.CostEstimate(
             flops=10 ** 6, bytes_accessed=4 * S, transcendentals=0),
         name="factor_and_finish",
@@ -548,16 +536,13 @@
                 order.append(step)
             step *= 2
         parts = [pass_on(part, order, 0) for part, order in zip(packed, orders)]
-        parts, later = barrier((parts, leaf_index))
-        sent = child_rows(later, child, row_count)
+        parts = barrier(parts)
         parts = [pass_on(part, order, 1) for part, order in zip(parts, orders)]
-        parts, sent, index = barrier((parts, sent, index))
+        parts, index = barrier((parts, index))
         for n in range(2, len(orders[0]) - 1):
             parts = [pass_on(part, order, n) for part, order in zip(parts, orders)]
-        parts, came, sent = barrier((parts, came, sent))
-        recv = lax.ppermute(sent, "leaf", swap)
+        parts, came = barrier((parts, came))
     else:
-        recv = lax.ppermute(child_rows(leaf_index, child, row_count), "leaf", swap)
         sources = [spread_pivot(cols, front_index, front_count, S // col_count)]
     piece = jnp.where(own, piece, came)
 
@@ -573,15 +558,15 @@
         sources = parts + [lax.ppermute(part, "leaf", swap) for part in parts]
     over = [across(part, 4) for part in held]
     cut = col_count // 2
-    u, x = first_step(place, sources)
+    u, x, sent = first_step(place, sources, child, row_count)
     u, x, sides = barrier((u, x, sides))
     crossed = [(across(xs[:cut], 2), across(ys[cut:], 1)) for xs, ys in sides]
     u, x = middle_step(1, u, x)
-    u, x, over = barrier((u, x, over))
+    u, x, over, crossed, sent = barrier((u, x, over, crossed, sent))
+    recv = lax.ppermute(sent, "leaf", swap)
     over_sides = [(across(part, 1), across(part, 2)) for part in over]
+    over_crossed = [(across(low, 4), across(high, 4)) for low, high in crossed]
     u, x = middle_step(2, u, x)
-    u, x, crossed = barrier((u, x, crossed))
-    over_crossed = [(across(low, 4), across(high, 4)) for low, high in crossed]
 
     early, late = [], []
     for group, first, alone, beside, cross in (

time: 132 us -> 132 us (level)
  starting transfers between devices: 35.1 us -> 41.4 us
  local copies, waits for them, and re-layouts: 6.76 us -> 2.39 us
  Pallas kernels: 61.2 us -> 58.7 us
    ppermute x9, starting transfers between devices: 12.8 us -> 18.6 us  [across(): lax.ppermute(value, 'front', [(f, f ^ bit) for f in range(front_count)])]
    unnamed x24 -> x16, local copies, waits for them, and re-layouts: 6.69 us -> 2.32 us
    ppermute x1, waiting for transfers between devices: 0.01 us -> 1.58 us  [per_device(): recv = lax.ppermute(sent, 'leaf', swap)]
    ppermute x2, waiting for transfers between devices: 2.64 us -> 1.12 us  [per_device(): sources = parts + [lax.ppermute(part, 'leaf', swap) for part in parts]]
    pallas_call x1, Pallas kernels: 24 us -> 22.5 us  [last_step(): pl.pallas_call(functools.partial(last_step_kernel, keys_of(early), late),...]
    pallas_call x2 -> x1, Pallas kernels: 13.7 us -> 12.6 us  [first_step(): pl.pallas_call(first_step_kernel, out_shape=[SQUARE] * 2 + [jax.ShapeDtyp...]
  transfers between devices with their start and end apart: 23 -> 23, of which waited for: 13 -> 16; matrix products, arithmetic and copies ran while one was open for 1% -> 0% of each run, Pallas kernels for 39% -> 37%
where the time goes in v2:
time: 132 us; the launch traced here: 131 us
  Pallas kernels  58.7 us (44%)
  starting transfers between devices  41.4 us (31%)
  waiting for transfers between devices  26.6 us (20%)
  local copies, waits for them, and re-layouts  2.39 us (2%)
    pallas_call x1, Pallas kernels, last_step(): pl.pallas_call(functools.partial(last_step_kernel, keys_of(early), late),...  22.5 us
    ppermute x9, starting transfers between devices, across(): lax.ppermute(value, 'front', [(f, f ^ bit) for f in range(front_count)])  18.6 us
    ppermute x8, starting transfers between devices, pass_on(): return part + lax.ppermute(part, 'front', [(f, f + steps[n]) for f in held])  15.8 us
    ppermute x8, waiting for transfers between devices, pass_on(): return part + lax.ppermute(part, 'front', [(f, f + steps[n]) for f in held])  14.5 us
    pallas_call x2, Pallas kernels, middle_step(): pl.pallas_call(functools.partial(middle_step_kernel, step), out_shape=[SQ...  13.1 us
    pallas_call x1, Pallas kernels, first_step(): pl.pallas_call(first_step_kernel, out_shape=[SQUARE] * 2 + [jax.ShapeDtyp...  12.6 us
    pallas_call x1, Pallas kernels, finish(): pl.pallas_call(functools.partial(finish_kernel, keys_of(parts)), out_shap...  6.08 us
    ppermute x1, starting transfers between devices, per_device(): came = lax.ppermute(piece, ('leaf', 'front'), pairs)  5.92 us
  transfers between devices with their start and end apart: 23, of which 16 were waited for; matrix products, arithmetic and copies ran while one was open for 0% of the time, Pallas kernels for 37%

profile of v2, /device:TPU:0, one launch (start us, length us, event | category | flops | bytes accessed | tf_op | source)
XLA Modules:
  0.0 130.9 jit_solution(14653502351676205128)
XLA Ops:
  0.7 3.4 %pivot_rows.1.mine_ref = f32[512,512]{1,0:T(8,128)} custom-call(s32[3]{0:T(128)} %pad_add_fusion.1.place, s32[48]{0:T(128)} %bitcast.14, f32[4096,512]{1,0:T(8,128)} %front_hbm.3, f32[6144,512]{1,0:T(8,128)} %bitcast.11), custom_call_target="tpu_custom_call" | custom-call | flops 1048576 | bytes 3145728 | tf_op jit(solution)/shard_map/pivot_rows/pallas_call | solution.py:113
  4.6 2.5 %collective-permute-done.other_ref = f32[512,512]{1,0:T(8,128)S(1)} collective-permute-done((f32[512,512]{1,0:T(8,128)}, f32[512,512]{1,0:T(8,128)S(1)}, u32[]{:S(2)}, u32[]{:S(2)}) %collective-permute-start) | collective-permute-done | bytes 1048608 | tf_op jit(solution)/shard_map/ppermute | solution.py:514
  10.3 5.9 %collective-permute-start.8 = (f32[512,512]{1,0:T(8,128)S(1)}, f32[512,512]{1,0:T(8,128)S(1)}, u32[]{:S(2)}, u32[]{:S(2)}) collective-permute-start(f32[512,512]{1,0:T(8,128)S(1)} %get-tuple-element.47), channel_id=1, source_target_pairs={{0,8},{1,9},{2,10},{3,11},{4,12},{5,13},{6,14},{7,15},{24,16},{25,... | collective-permute-start | bytes 3145736 | tf_op jit(solution)/shard_map/ppermute | solution.py:518
  17.6 3.4 %collective-permute-start.2 = (f32[320,128]{1,0:T(8,128)S(1)}, f32[320,128]{1,0:T(8,128)S(1)}, u32[]{:S(2)}, u32[]{:S(2)}) collective-permute-start(f32[320,128]{1,0:T(8,128)S(1)} %get-tuple-element.41), channel_id=1, source_target_pairs={{0,2},{16,18}} | collective-permute-start | bytes 491528 | tf_op jit(solution)/shard_map/ppermute | solution.py:497
  22.4 2.5 %collective-permute-done.2 = f32[320,128]{1,0:T(8,128)S(1)} collective-permute-done((f32[320,128]{1,0:T(8,128)S(1)}, f32[320,128]{1,0:T(8,128)S(1)}, u32[]{:S(2)}, u32[]{:S(2)}) %collective-permute-start.2) | collective-permute-done | bytes 163872 | tf_op jit(solution)/shard_map/ppermute | solution.py:497
  26.2 4.4 %collective-permute-start.4 = (f32[320,128]{1,0:T(8,128)S(1)}, f32[320,128]{1,0:T(8,128)S(1)}, u32[]{:S(2)}, u32[]{:S(2)}) collective-permute-start(f32[320,128]{1,0:T(8,128)S(1)} %add.60), channel_id=1, source_target_pairs={{0,1},{2,3},{16,17},{18,19}} | collective-permute-start | bytes 491528 | tf_op jit(solution)/shard_map/ppermute | solution.py:497
  31.9 1.6 %collective-permute-done.4 = f32[320,128]{1,0:T(8,128)S(1)} collective-permute-done((f32[320,128]{1,0:T(8,128)S(1)}, f32[320,128]{1,0:T(8,128)S(1)}, u32[]{:S(2)}, u32[]{:S(2)}) %collective-permute-start.4) | collective-permute-done | bytes 163872 | tf_op jit(solution)/shard_map/ppermute | solution.py:497
  37.5 2.7 %collective-permute-done.7 = f32[320,128]{1,0:T(8,128)S(1)} collective-permute-done((f32[320,128]{1,0:T(8,128)S(1)}, f32[320,128]{1,0:T(8,128)S(1)}, u32[]{:S(2)}, u32[]{:S(2)}) %collective-permute-start.7) | collective-permute-done | bytes 163872 | tf_op jit(solution)/shard_map/ppermute | solution.py:497
  40.2 1.7 %collective-permute-done.6 = f32[320,128]{1,0:T(8,128)S(1)} collective-permute-done((f32[320,128]{1,0:T(8,128)S(1)}, f32[320,128]{1,0:T(8,128)S(1)}, u32[]{:S(2)}, u32[]{:S(2)}) %collective-permute-start.6) | collective-permute-done | bytes 163872 | tf_op jit(solution)/shard_map/ppermute | solution.py:497
  46.2 1.5 %collective-permute-start.9 = (f32[320,128]{1,0:T(8,128)S(1)}, f32[320,128]{1,0:T(8,128)S(1)}, u32[]{:S(2)}, u32[]{:S(2)}) collective-permute-start(f32[320,128]{1,0:T(8,128)S(1)} %add.65), channel_id=1, source_target_pairs={{0,8},{1,9},{2,10},{3,11},{4,12},{5,13},{6,14},{7,15},{16,24},{17,... | collective-permute-start | bytes 491528 | tf_op jit(solution)/shard_map/ppermute | solution.py:497
  47.7 1.7 %collective-permute-done.10 = f32[320,128]{1,0:T(8,128)S(1)} collective-permute-done((f32[320,128]{1,0:T(8,128)S(1)}, f32[320,128]{1,0:T(8,128)S(1)}, u32[]{:S(2)}, u32[]{:S(2)}) %collective-permute-start.10) | collective-permute-done | bytes 163872 | tf_op jit(solution)/shard_map/ppermute | solution.py:497
  49.5 1.7 %collective-permute-done.9 = f32[320,128]{1,0:T(8,128)S(1)} collective-permute-done((f32[320,128]{1,0:T(8,128)S(1)}, f32[320,128]{1,0:T(8,128)S(1)}, u32[]{:S(2)}, u32[]{:S(2)}) %collective-permute-start.9) | collective-permute-done | bytes 163872 | tf_op jit(solution)/shard_map/ppermute | solution.py:497
  51.2 8.5 %collective-permute-start.15 = (f32[512,512]{1,0:T(8,128)S(1)}, f32[512,512]{1,0:T(8,128)S(1)}, u32[]{:S(2)}, u32[]{:S(2)}) collective-permute-start(f32[512,512]{1,0:T(8,128)S(1)} %broadcast_select_fusion.refs_0_), channel_id=1, source_target_pairs={{0,4},{1,5},{2,6},{3,7},{4,0},{5,1},{6,2},{7,3},{8,12},{9,13},{10,... | collective-permute-start | bytes 3145736 | tf_op jit(solution)/shard_map/ppermute | solution.py:528
  61.4 12.6 %factor_step.3 = (f32[512,512]{1,0:T(8,128)S(1)}, f32[512,512]{1,0:T(8,128)S(1)}, f32[4096,512]{1,0:T(8,128)}) custom-call(s32[3]{0:T(128)S(1)} %copy-done.2, f32[6144,512]{1,0:T(8,128)} %bitcast.12, f32[320,128]{1,0:T(8,128)S(1)} %add.67.refs_0_, f32[320,128]{1,0:T(8,128)S(1)} %add.68.refs_1_, f32[320,128]{1,0:T(8,128)S(1)} %collective-permute-done.11.refs_2_, ...), custom_call_target="tpu_custom_call" | custom-call | flops 1000000 | bytes 2048 | tf_op jit(solution)/shard_map/factor_step/pallas_call | solution.py:252
  74.6 1.6 %collective-permute-start.17 = (f32[256,512]{1,0:T(8,128)S(1)}, f32[256,512]{1,0:T(8,128)S(1)}, u32[]{:S(2)}, u32[]{:S(2)}) collective-permute-start(f32[256,512]{1,0:T(8,128)S(1)} %slice.7), channel_id=1, source_target_pairs={{0,1},{1,0},{2,3},{3,2},{4,5},{5,4},{6,7},{7,6},{8,9},{9,8},{10,11... | collective-permute-start | bytes 1572872 | tf_op jit(solution)/shard_map/ppermute | solution.py:528
  76.2 6.5 %factor_step.4 = (f32[512,512]{1,0:T(8,128)S(1)}, f32[512,512]{1,0:T(8,128)S(1)}) custom-call(f32[512,512]{1,0:T(8,128)S(1)} %get-tuple-element.55.u_in, f32[512,512]{1,0:T(8,128)S(1)} %get-tuple-element.56.x_in), custom_call_target="tpu_custom_call" | custom-call | flops 1000000 | bytes 2048 | tf_op jit(solution)/shard_map/factor_step/pallas_call | solution.py:265
  83.1 5.2 %collective-permute-done.16.refs_3_ = f32[256,512]{1,0:T(8,128)S(1)} collective-permute-done((f32[256,512]{1,0:T(8,128)S(1)}, f32[256,512]{1,0:T(8,128)S(1)}, u32[]{:S(2)}, u32[]{:S(2)}) %collective-permute-start.16) | collective-permute-done | bytes 524320 | tf_op jit(solution)/shard_map/ppermute | solution.py:528
  88.5 1.6 %collective-permute-start.19 = (f32[512,512]{1,0:T(8,128)S(1)}, f32[512,512]{1,0:T(8,128)S(1)}, u32[]{:S(2)}, u32[]{:S(2)}) collective-permute-start(f32[512,512]{1,0:T(8,128)S(1)} %collective-permute-done.15.refs_5_), channel_id=1, source_target_pairs={{0,1},{1,0},{2,3},{3,2},{4,5},{5,4},{6,7},{7,6},{8,9},{9,8},{10,11... | collective-permute-start | bytes 3145736 | tf_op jit(solution)/shard_map/ppermute | solution.py:528
  90.1 1.7 %collective-permute-start.20 = (f32[512,512]{1,0:T(8,128)S(1)}, f32[512,512]{1,0:T(8,128)S(1)}, u32[]{:S(2)}, u32[]{:S(2)}) collective-permute-start(f32[512,512]{1,0:T(8,128)S(1)} %collective-permute-done.15.refs_5_), channel_id=1, source_target_pairs={{0,2},{1,3},{2,0},{3,1},{4,6},{5,7},{6,4},{7,5},{8,10},{9,11},{10,... | collective-permute-start | bytes 3145736 | tf_op jit(solution)/shard_map/ppermute | solution.py:528
  91.9 1.9 %collective-permute-start.22 = (f32[256,512]{1,0:T(8,128)S(1)}, f32[256,512]{1,0:T(8,128)S(1)}, u32[]{:S(2)}, u32[]{:S(2)}) collective-permute-start(f32[256,512]{1,0:T(8,128)S(1)} %collective-permute-done.17.refs_4_), channel_id=1, source_target_pairs={{0,4},{1,5},{2,6},{3,7},{4,0},{5,1},{6,2},{7,3},{8,12},{9,13},{10,... | collective-permute-start | bytes 1572872 | tf_op jit(solution)/shard_map/ppermute | solution.py:528
  93.8 6.6 %factor_step.5 = (f32[512,512]{1,0:T(8,128)S(1)}, f32[512,512]{1,0:T(8,128)S(1)}) custom-call(f32[512,512]{1,0:T(8,128)S(1)} %get-tuple-element.63.u_in, f32[512,512]{1,0:T(8,128)S(1)} %get-tuple-element.64.x_in), custom_call_target="tpu_custom_call" | custom-call | flops 1000000 | bytes 2048 | tf_op jit(solution)/shard_map/factor_step/pallas_call | solution.py:265
  100.4 1.6 %collective-permute-done.18.recv_hbm = f32[4096,512]{1,0:T(8,128)} collective-permute-done((f32[4096,512]{1,0:T(8,128)}, f32[4096,512]{1,0:T(8,128)}, u32[]{:S(2)}, u32[]{:S(2)}) %collective-permute-start.18) | collective-permute-done | bytes 8388640 | tf_op jit(solution)/shard_map/ppermute | solution.py:566
  102.0 22.5 %factor_and_finish.1 = (f32[4096,512]{1,0:T(8,128)}, f32[512,512]{1,0:T(8,128)S(1)}, f32[512,512]{1,0:T(8,128)S(1)}) custom-call(s32[3]{0:T(128)S(1)} %copy-done.2, s32[4,32]{1,0:T(4,128)S(1)} %pad_add_fusion.index, f32[512,512]{1,0:T(8,128)S(1)} %get-tuple-element.65.u_in, f32[512,512]{1,0:T(8,128)S(1)} %get-tuple-element.66.x_in, f32[512,512]{1,0:T(8,128)} %copy-done.1, ...), custom_call_target="tpu_custom_call" | custom-call | flops 1000000 | bytes 2048 | tf_op jit(solution)/shard_map/factor_and_finish/pallas_call | solution.py:385
  124.6 6.1 %finish.1 = f32[4096,512]{1,0:T(8,128)} custom-call(s32[3]{0:T(128)S(1)} %copy-done.2, f32[4096,512]{1,0:T(8,128)} %get-tuple-element.72.base_hbm, f32[512,512]{1,0:T(8,128)S(1)} %get-tuple-element.73.mult_ref, f32[512,512]{1,0:T(8,128)S(1)} %get-tuple-element.74.top_ref, ...), custom_call_target="tpu_custom_call", output_to_operand_aliasing={{}: (1, {})} | custom-call | flops 2415919104 | bytes 9437184 | tf_op jit(solution)/shard_map/finish/pallas_call | solution.py:439
  (62 shorter events, 20.7 us)
Async XLA Ops:
  4.1 3.0 %collective-permute-start = (f32[512,512]{1,0:T(8,128)}, f32[512,512]{1,0:T(8,128)S(1)}, u32[]{:S(2)}, u32[]{:S(2)}) collective-permute-start(f32[512,512]{1,0:T(8,128)} %pivot_rows.1.mine_ref), channel_id=1, source_target_pairs={{0,16},{16,0},{1,17},{17,1},{2,18},{18,2},{3,19},{19,3},{4,20},{20... | collective-permute-start | bytes 3145736 | tf_op jit(solution)/shard_map/ppermute | solution.py:514
  10.3 31.7 %collective-permute-start.8 = (f32[512,512]{1,0:T(8,128)S(1)}, f32[512,512]{1,0:T(8,128)S(1)}, u32[]{:S(2)}, u32[]{:S(2)}) collective-permute-start(f32[512,512]{1,0:T(8,128)S(1)} %get-tuple-element.47), channel_id=1, source_target_pairs={{0,8},{1,9},{2,10},{3,11},{4,12},{5,13},{6,14},{7,15},{24,16},{25,... | collective-permute-start | bytes 3145736 | tf_op jit(solution)/shard_map/ppermute | solution.py:518
  16.2 1.2 collective-permute-start.5
  17.6 7.2 %collective-permute-start.2 = (f32[320,128]{1,0:T(8,128)S(1)}, f32[320,128]{1,0:T(8,128)S(1)}, u32[]{:S(2)}, u32[]{:S(2)}) collective-permute-start(f32[320,128]{1,0:T(8,128)S(1)} %get-tuple-element.41), channel_id=1, source_target_pairs={{0,2},{16,18}} | collective-permute-start | bytes 491528 | tf_op jit(solution)/shard_map/ppermute | solution.py:497
  21.1 5.1 %collective-permute-start.1 = (f32[320,128]{1,0:T(8,128)S(1)}, f32[320,128]{1,0:T(8,128)S(1)}, u32[]{:S(2)}, u32[]{:S(2)}) collective-permute-start(f32[320,128]{1,0:T(8,128)S(1)} %get-tuple-element.40), channel_id=1, source_target_pairs={{0,1},{16,17}} | collective-permute-start | bytes 491528 | tf_op jit(solution)/shard_map/ppermute | solution.py:497
  26.2 7.4 %collective-permute-start.4 = (f32[320,128]{1,0:T(8,128)S(1)}, f32[320,128]{1,0:T(8,128)S(1)}, u32[]{:S(2)}, u32[]{:S(2)}) collective-permute-start(f32[320,128]{1,0:T(8,128)S(1)} %add.60), channel_id=1, source_target_pairs={{0,1},{2,3},{16,17},{18,19}} | collective-permute-start | bytes 491528 | tf_op jit(solution)/shard_map/ppermute | solution.py:497
  30.6 4.3 %collective-permute-start.3 = (f32[320,128]{1,0:T(8,128)S(1)}, f32[320,128]{1,0:T(8,128)S(1)}, u32[]{:S(2)}, u32[]{:S(2)}) collective-permute-start(f32[320,128]{1,0:T(8,128)S(1)} %add.59), channel_id=1, source_target_pairs={{0,2},{1,3},{16,18},{17,19}} | collective-permute-start | bytes 491528 | tf_op jit(solution)/shard_map/ppermute | solution.py:497
  34.9 5.3 %collective-permute-start.7 = (f32[320,128]{1,0:T(8,128)S(1)}, f32[320,128]{1,0:T(8,128)S(1)}, u32[]{:S(2)}, u32[]{:S(2)}) collective-permute-start(f32[320,128]{1,0:T(8,128)S(1)} %add.62), channel_id=1, source_target_pairs={{0,4},{2,6},{1,5},{3,7},{16,20},{18,22},{17,21},{19,23}} | collective-permute-start | bytes 491528 | tf_op jit(solution)/shard_map/ppermute | solution.py:497
  36.2 5.7 %collective-permute-start.6 = (f32[320,128]{1,0:T(8,128)S(1)}, f32[320,128]{1,0:T(8,128)S(1)}, u32[]{:S(2)}, u32[]{:S(2)}) collective-permute-start(f32[320,128]{1,0:T(8,128)S(1)} %add.61), channel_id=1, source_target_pairs={{0,4},{1,5},{2,6},{3,7},{16,20},{17,21},{18,22},{19,23}} | collective-permute-start | bytes 491528 | tf_op jit(solution)/shard_map/ppermute | solution.py:497
  42.2 40.6 %copy-start.3 = (f32[512,512]{1,0:T(8,128)}, f32[512,512]{1,0:T(8,128)S(1)}, u32[]{:S(2)}) copy-start(f32[512,512]{1,0:T(8,128)S(1)} %broadcast_select_fusion.refs_0_) | copy-start | bytes 3145732
  42.2 31.8 %collective-permute-start.13 = (f32[512,512]{1,0:T(8,128)S(1)}, f32[512,512]{1,0:T(8,128)S(1)}, u32[]{:S(2)}, u32[]{:S(2)}) collective-permute-start(f32[512,512]{1,0:T(8,128)S(1)} %broadcast_select_fusion.refs_0_), channel_id=1, source_target_pairs={{0,1},{1,0},{2,3},{3,2},{4,5},{5,4},{6,7},{7,6},{8,9},{9,8},{10,11... | collective-permute-start | bytes 3145736 | tf_op jit(solution)/shard_map/ppermute | solution.py:528
  43.6 30.4 %collective-permute-start.14 = (f32[512,512]{1,0:T(8,128)S(1)}, f32[512,512]{1,0:T(8,128)S(1)}, u32[]{:S(2)}, u32[]{:S(2)}) collective-permute-start(f32[512,512]{1,0:T(8,128)S(1)} %broadcast_select_fusion.refs_0_), channel_id=1, source_target_pairs={{0,2},{1,3},{2,0},{3,1},{4,6},{5,7},{6,4},{7,5},{8,10},{9,11},{10,... | collective-permute-start | bytes 3145736 | tf_op jit(solution)/shard_map/ppermute | solution.py:528
  45.0 4.5 %collective-permute-start.10 = (f32[320,128]{1,0:T(8,128)S(1)}, f32[320,128]{1,0:T(8,128)S(1)}, u32[]{:S(2)}, u32[]{:S(2)}) collective-permute-start(f32[320,128]{1,0:T(8,128)S(1)} %add.66), channel_id=1, source_target_pairs={{0,8},{2,10},{1,9},{3,11},{4,12},{6,14},{5,13},{7,15},{16,24},{18,... | collective-permute-start | bytes 491528 | tf_op jit(solution)/shard_map/ppermute | solution.py:497
  46.2 5.0 %collective-permute-start.9 = (f32[320,128]{1,0:T(8,128)S(1)}, f32[320,128]{1,0:T(8,128)S(1)}, u32[]{:S(2)}, u32[]{:S(2)}) collective-permute-start(f32[320,128]{1,0:T(8,128)S(1)} %add.65), channel_id=1, source_target_pairs={{0,8},{1,9},{2,10},{3,11},{4,12},{5,13},{6,14},{7,15},{16,24},{17,... | collective-permute-start | bytes 491528 | tf_op jit(solution)/shard_map/ppermute | solution.py:497
  51.2 31.8 %collective-permute-start.15 = (f32[512,512]{1,0:T(8,128)S(1)}, f32[512,512]{1,0:T(8,128)S(1)}, u32[]{:S(2)}, u32[]{:S(2)}) collective-permute-start(f32[512,512]{1,0:T(8,128)S(1)} %broadcast_select_fusion.refs_0_), channel_id=1, source_target_pairs={{0,4},{1,5},{2,6},{3,7},{4,0},{5,1},{6,2},{7,3},{8,12},{9,13},{10,... | collective-permute-start | bytes 3145736 | tf_op jit(solution)/shard_map/ppermute | solution.py:528
  59.7 1.4 %collective-permute-start.11 = (f32[320,128]{1,0:T(8,128)S(1)}, f32[320,128]{1,0:T(8,128)S(1)}, u32[]{:S(2)}, u32[]{:S(2)}) collective-permute-start(f32[320,128]{1,0:T(8,128)S(1)} %add.67.refs_0_), channel_id=1, source_target_pairs={{0,16},{16,0},{1,17},{17,1},{2,18},{18,2},{3,19},{19,3},{4,20},{20... | collective-permute-start | bytes 491528 | tf_op jit(solution)/shard_map/ppermute | solution.py:558
  59.7 1.6 %collective-permute-start.12 = (f32[320,128]{1,0:T(8,128)S(1)}, f32[320,128]{1,0:T(8,128)S(1)}, u32[]{:S(2)}, u32[]{:S(2)}) collective-permute-start(f32[320,128]{1,0:T(8,128)S(1)} %add.68.refs_1_), channel_id=1, source_target_pairs={{0,16},{16,0},{1,17},{17,1},{2,18},{18,2},{3,19},{19,3},{4,20},{20... | collective-permute-start | bytes 491528 | tf_op jit(solution)/shard_map/ppermute | solution.py:558
  74.1 14.2 %collective-permute-start.16 = (f32[256,512]{1,0:T(8,128)S(1)}, f32[256,512]{1,0:T(8,128)S(1)}, u32[]{:S(2)}, u32[]{:S(2)}) collective-permute-start(f32[256,512]{1,0:T(8,128)S(1)} %slice.6), channel_id=1, source_target_pairs={{0,2},{1,3},{2,0},{3,1},{4,6},{5,7},{6,4},{7,5},{8,10},{9,11},{10,... | collective-permute-start | bytes 1572872 | tf_op jit(solution)/shard_map/ppermute | solution.py:528
  74.6 13.9 %collective-permute-start.17 = (f32[256,512]{1,0:T(8,128)S(1)}, f32[256,512]{1,0:T(8,128)S(1)}, u32[]{:S(2)}, u32[]{:S(2)}) collective-permute-start(f32[256,512]{1,0:T(8,128)S(1)} %slice.7), channel_id=1, source_target_pairs={{0,1},{1,0},{2,3},{3,2},{4,5},{5,4},{6,7},{7,6},{8,9},{9,8},{10,11... | collective-permute-start | bytes 1572872 | tf_op jit(solution)/shard_map/ppermute | solution.py:528
  88.5 13.5 %collective-permute-start.18 = (f32[4096,512]{1,0:T(8,128)}, f32[4096,512]{1,0:T(8,128)}, u32[]{:S(2)}, u32[]{:S(2)}) collective-permute-start(f32[4096,512]{1,0:T(8,128)} %get-tuple-element.68), channel_id=1, source_target_pairs={{0,16},{16,0},{1,17},{17,1},{2,18},{18,2},{3,19},{19,3},{4,20},{20... | collective-permute-start | bytes 25165832 | tf_op jit(solution)/shard_map/ppermute | solution.py:566
  88.5 36.1 %collective-permute-start.19 = (f32[512,512]{1,0:T(8,128)S(1)}, f32[512,512]{1,0:T(8,128)S(1)}, u32[]{:S(2)}, u32[]{:S(2)}) collective-permute-start(f32[512,512]{1,0:T(8,128)S(1)} %collective-permute-done.15.refs_5_), channel_id=1, source_target_pairs={{0,1},{1,0},{2,3},{3,2},{4,5},{5,4},{6,7},{7,6},{8,9},{9,8},{10,11... | collective-permute-start | bytes 3145736 | tf_op jit(solution)/shard_map/ppermute | solution.py:528
  90.1 34.5 %collective-permute-start.20 = (f32[512,512]{1,0:T(8,128)S(1)}, f32[512,512]{1,0:T(8,128)S(1)}, u32[]{:S(2)}, u32[]{:S(2)}) collective-permute-start(f32[512,512]{1,0:T(8,128)S(1)} %collective-permute-done.15.refs_5_), channel_id=1, source_target_pairs={{0,2},{1,3},{2,0},{3,1},{4,6},{5,7},{6,4},{7,5},{8,10},{9,11},{10,... | collective-permute-start | bytes 3145736 | tf_op jit(solution)/shard_map/ppermute | solution.py:528
  91.8 32.8 %collective-permute-start.21 = (f32[256,512]{1,0:T(8,128)S(1)}, f32[256,512]{1,0:T(8,128)S(1)}, u32[]{:S(2)}, u32[]{:S(2)}) collective-permute-start(f32[256,512]{1,0:T(8,128)S(1)} %collective-permute-done.16.refs_3_), channel_id=1, source_target_pairs={{0,4},{1,5},{2,6},{3,7},{4,0},{5,1},{6,2},{7,3},{8,12},{9,13},{10,... | collective-permute-start | bytes 1572872 | tf_op jit(solution)/shard_map/ppermute | solution.py:528
  91.9 32.7 %collective-permute-start.22 = (f32[256,512]{1,0:T(8,128)S(1)}, f32[256,512]{1,0:T(8,128)S(1)}, u32[]{:S(2)}, u32[]{:S(2)}) collective-permute-start(f32[256,512]{1,0:T(8,128)S(1)} %collective-permute-done.17.refs_4_), channel_id=1, source_target_pairs={{0,4},{1,5},{2,6},{3,7},{4,0},{5,1},{6,2},{7,3},{8,12},{9,13},{10,... | collective-permute-start | bytes 1572872 | tf_op jit(solution)/shard_map/ppermute | solution.py:528
  (7 other events, 99.2 us)

commit v3 on v2

--- a/solution.py
+++ b/solution.py
@@ -172,8 +172,8 @@
 def factor_step(step, u_ref, x_ref, between=lambda: None):
     rows = slice(step * BLK, (step + 1) * BLK)
     done, rest = slice(0, (step + 1) * BLK), slice((step + 1) * BLK, S)
+    between()
     block, inverse, pivots = eliminate_block(u_ref[rows, rows])
-    between()
     scale = lax.rsqrt(pivots)
     scale = scale * (1.5 - 0.5 * pivots * scale * scale)
     r = lax.broadcasted_iota(jnp.int32, (BLK, BLK), 0)
@@ -352,7 +352,7 @@
     mult_ref[...] = exact_dot(x_ref[...], right, ((0,), (0,)))
 
     outs = []
-    for n in list(range(len(early), len(parts))) + list(range(len(early))):
+    for n in range(len(parts)):
         for copy in started[n]:
             copy.wait()
         for j, size in subs(n):

time: 132 us -> 129 us (0.977)
  Pallas kernels: 58.7 us -> 55.9 us
    pallas_call x1, Pallas kernels: 22.5 us -> 19.7 us  [last_step(): pl.pallas_call(functools.partial(last_step_kernel, keys_of(early), late),...]
  transfers between devices with their start and end apart: 23 -> 23, of which waited for: 16 -> 16; matrix products, arithmetic and copies ran while one was open for 0% -> 0% of each run, Pallas kernels for 37% -> 36%
where the time goes in v3:
time: 129 us; the launch traced here: 128 us
  Pallas kernels  55.9 us (43%)
  starting transfers between devices  41.4 us (32%)
  waiting for transfers between devices  26.6 us (21%)
  local copies, waits for them, and re-layouts  2.39 us (2%)
    pallas_call x1, Pallas kernels, last_step(): pl.pallas_call(functools.partial(last_step_kernel, keys_of(early), late),...  19.7 us
    ppermute x9, starting transfers between devices, across(): lax.ppermute(value, 'front', [(f, f ^ bit) for f in range(front_count)])  18.6 us
    ppermute x8, starting transfers between devices, pass_on(): return part + lax.ppermute(part, 'front', [(f, f + steps[n]) for f in held])  15.8 us
    ppermute x8, waiting for transfers between devices, pass_on(): return part + lax.ppermute(part, 'front', [(f, f + steps[n]) for f in held])  14.5 us
    pallas_call x2, Pallas kernels, middle_step(): pl.pallas_call(functools.partial(middle_step_kernel, step), out_shape=[SQ...  13.1 us
    pallas_call x1, Pallas kernels, first_step(): pl.pallas_call(first_step_kernel, out_shape=[SQUARE] * 2 + [jax.ShapeDtyp...  12.7 us
    pallas_call x1, Pallas kernels, finish(): pl.pallas_call(functools.partial(finish_kernel, keys_of(parts)), out_shap...  6.09 us
    ppermute x1, starting transfers between devices, per_device(): came = lax.ppermute(piece, ('leaf', 'front'), pairs)  5.92 us
  transfers between devices with their start and end apart: 23, of which 16 were waited for; matrix products, arithmetic and copies ran while one was open for 0% of the time, Pallas kernels for 36%

profile of v3, /device:TPU:0, one launch (start us, length us, event | category | flops | bytes accessed | tf_op | source)
XLA Modules:
  0.0 128.2 jit_solution(7279858156105023781)
XLA Ops:
  0.7 3.4 %pivot_rows.1.mine_ref = f32[512,512]{1,0:T(8,128)} custom-call(s32[3]{0:T(128)} %pad_add_fusion.1.place, s32[48]{0:T(128)} %bitcast.14, f32[4096,512]{1,0:T(8,128)} %front_hbm.3, f32[6144,512]{1,0:T(8,128)} %bitcast.11), custom_call_target="tpu_custom_call" | custom-call | flops 1048576 | bytes 3145728 | tf_op jit(solution)/shard_map/pivot_rows/pallas_call | solution.py:113
  4.6 2.5 %collective-permute-done.other_ref = f32[512,512]{1,0:T(8,128)S(1)} collective-permute-done((f32[512,512]{1,0:T(8,128)}, f32[512,512]{1,0:T(8,128)S(1)}, u32[]{:S(2)}, u32[]{:S(2)}) %collective-permute-start) | collective-permute-done | bytes 1048608 | tf_op jit(solution)/shard_map/ppermute | solution.py:514
  10.3 5.9 %collective-permute-start.8 = (f32[512,512]{1,0:T(8,128)S(1)}, f32[512,512]{1,0:T(8,128)S(1)}, u32[]{:S(2)}, u32[]{:S(2)}) collective-permute-start(f32[512,512]{1,0:T(8,128)S(1)} %get-tuple-element.47), channel_id=1, source_target_pairs={{0,8},{1,9},{2,10},{3,11},{4,12},{5,13},{6,14},{7,15},{24,16},{25,... | collective-permute-start | bytes 3145736 | tf_op jit(solution)/shard_map/ppermute | solution.py:518
  17.6 3.4 %collective-permute-start.2 = (f32[320,128]{1,0:T(8,128)S(1)}, f32[320,128]{1,0:T(8,128)S(1)}, u32[]{:S(2)}, u32[]{:S(2)}) collective-permute-start(f32[320,128]{1,0:T(8,128)S(1)} %get-tuple-element.41), channel_id=1, source_target_pairs={{0,2},{16,18}} | collective-permute-start | bytes 491528 | tf_op jit(solution)/shard_map/ppermute | solution.py:497
  22.4 2.5 %collective-permute-done.2 = f32[320,128]{1,0:T(8,128)S(1)} collective-permute-done((f32[320,128]{1,0:T(8,128)S(1)}, f32[320,128]{1,0:T(8,128)S(1)}, u32[]{:S(2)}, u32[]{:S(2)}) %collective-permute-start.2) | collective-permute-done | bytes 163872 | tf_op jit(solution)/shard_map/ppermute | solution.py:497
  26.2 4.4 %collective-permute-start.4 = (f32[320,128]{1,0:T(8,128)S(1)}, f32[320,128]{1,0:T(8,128)S(1)}, u32[]{:S(2)}, u32[]{:S(2)}) collective-permute-start(f32[320,128]{1,0:T(8,128)S(1)} %add.60), channel_id=1, source_target_pairs={{0,1},{2,3},{16,17},{18,19}} | collective-permute-start | bytes 491528 | tf_op jit(solution)/shard_map/ppermute | solution.py:497
  31.9 1.6 %collective-permute-done.4 = f32[320,128]{1,0:T(8,128)S(1)} collective-permute-done((f32[320,128]{1,0:T(8,128)S(1)}, f32[320,128]{1,0:T(8,128)S(1)}, u32[]{:S(2)}, u32[]{:S(2)}) %collective-permute-start.4) | collective-permute-done | bytes 163872 | tf_op jit(solution)/shard_map/ppermute | solution.py:497
  37.5 2.7 %collective-permute-done.7 = f32[320,128]{1,0:T(8,128)S(1)} collective-permute-done((f32[320,128]{1,0:T(8,128)S(1)}, f32[320,128]{1,0:T(8,128)S(1)}, u32[]{:S(2)}, u32[]{:S(2)}) %collective-permute-start.7) | collective-permute-done | bytes 163872 | tf_op jit(solution)/shard_map/ppermute | solution.py:497
  40.2 1.7 %collective-permute-done.6 = f32[320,128]{1,0:T(8,128)S(1)} collective-permute-done((f32[320,128]{1,0:T(8,128)S(1)}, f32[320,128]{1,0:T(8,128)S(1)}, u32[]{:S(2)}, u32[]{:S(2)}) %collective-permute-start.6) | collective-permute-done | bytes 163872 | tf_op jit(solution)/shard_map/ppermute | solution.py:497
  46.2 1.5 %collective-permute-start.9 = (f32[320,128]{1,0:T(8,128)S(1)}, f32[320,128]{1,0:T(8,128)S(1)}, u32[]{:S(2)}, u32[]{:S(2)}) collective-permute-start(f32[320,128]{1,0:T(8,128)S(1)} %add.65), channel_id=1, source_target_pairs={{0,8},{1,9},{2,10},{3,11},{4,12},{5,13},{6,14},{7,15},{16,24},{17,... | collective-permute-start | bytes 491528 | tf_op jit(solution)/shard_map/ppermute | solution.py:497
  47.7 1.7 %collective-permute-done.10 = f32[320,128]{1,0:T(8,128)S(1)} collective-permute-done((f32[320,128]{1,0:T(8,128)S(1)}, f32[320,128]{1,0:T(8,128)S(1)}, u32[]{:S(2)}, u32[]{:S(2)}) %collective-permute-start.10) | collective-permute-done | bytes 163872 | tf_op jit(solution)/shard_map/ppermute | solution.py:497
  49.5 1.7 %collective-permute-done.9 = f32[320,128]{1,0:T(8,128)S(1)} collective-permute-done((f32[320,128]{1,0:T(8,128)S(1)}, f32[320,128]{1,0:T(8,128)S(1)}, u32[]{:S(2)}, u32[]{:S(2)}) %collective-permute-start.9) | collective-permute-done | bytes 163872 | tf_op jit(solution)/shard_map/ppermute | solution.py:497
  51.2 8.5 %collective-permute-start.15 = (f32[512,512]{1,0:T(8,128)S(1)}, f32[512,512]{1,0:T(8,128)S(1)}, u32[]{:S(2)}, u32[]{:S(2)}) collective-permute-start(f32[512,512]{1,0:T(8,128)S(1)} %broadcast_select_fusion.refs_0_), channel_id=1, source_target_pairs={{0,4},{1,5},{2,6},{3,7},{4,0},{5,1},{6,2},{7,3},{8,12},{9,13},{10,... | collective-permute-start | bytes 3145736 | tf_op jit(solution)/shard_map/ppermute | solution.py:528
  61.4 12.7 %factor_step.3 = (f32[512,512]{1,0:T(8,128)S(1)}, f32[512,512]{1,0:T(8,128)S(1)}, f32[4096,512]{1,0:T(8,128)}) custom-call(s32[3]{0:T(128)S(1)} %copy-done.2, f32[6144,512]{1,0:T(8,128)} %bitcast.12, f32[320,128]{1,0:T(8,128)S(1)} %add.67.refs_0_, f32[320,128]{1,0:T(8,128)S(1)} %add.68.refs_1_, f32[320,128]{1,0:T(8,128)S(1)} %collective-permute-done.11.refs_2_, ...), custom_call_target="tpu_custom_call" | custom-call | flops 1000000 | bytes 2048 | tf_op jit(solution)/shard_map/factor_step/pallas_call | solution.py:252
  74.7 1.6 %collective-permute-start.17 = (f32[256,512]{1,0:T(8,128)S(1)}, f32[256,512]{1,0:T(8,128)S(1)}, u32[]{:S(2)}, u32[]{:S(2)}) collective-permute-start(f32[256,512]{1,0:T(8,128)S(1)} %slice.7), channel_id=1, source_target_pairs={{0,1},{1,0},{2,3},{3,2},{4,5},{5,4},{6,7},{7,6},{8,9},{9,8},{10,11... | collective-permute-start | bytes 1572872 | tf_op jit(solution)/shard_map/ppermute | solution.py:528
  76.3 6.5 %factor_step.4 = (f32[512,512]{1,0:T(8,128)S(1)}, f32[512,512]{1,0:T(8,128)S(1)}) custom-call(f32[512,512]{1,0:T(8,128)S(1)} %get-tuple-element.55.u_in, f32[512,512]{1,0:T(8,128)S(1)} %get-tuple-element.56.x_in), custom_call_target="tpu_custom_call" | custom-call | flops 1000000 | bytes 2048 | tf_op jit(solution)/shard_map/factor_step/pallas_call | solution.py:265
  83.1 5.3 %collective-permute-done.16.refs_3_ = f32[256,512]{1,0:T(8,128)S(1)} collective-permute-done((f32[256,512]{1,0:T(8,128)S(1)}, f32[256,512]{1,0:T(8,128)S(1)}, u32[]{:S(2)}, u32[]{:S(2)}) %collective-permute-start.16) | collective-permute-done | bytes 524320 | tf_op jit(solution)/shard_map/ppermute | solution.py:528
  88.6 1.6 %collective-permute-start.19 = (f32[512,512]{1,0:T(8,128)S(1)}, f32[512,512]{1,0:T(8,128)S(1)}, u32[]{:S(2)}, u32[]{:S(2)}) collective-permute-start(f32[512,512]{1,0:T(8,128)S(1)} %collective-permute-done.15.refs_5_), channel_id=1, source_target_pairs={{0,1},{1,0},{2,3},{3,2},{4,5},{5,4},{6,7},{7,6},{8,9},{9,8},{10,11... | collective-permute-start | bytes 3145736 | tf_op jit(solution)/shard_map/ppermute | solution.py:528
  90.1 1.7 %collective-permute-start.20 = (f32[512,512]{1,0:T(8,128)S(1)}, f32[512,512]{1,0:T(8,128)S(1)}, u32[]{:S(2)}, u32[]{:S(2)}) collective-permute-start(f32[512,512]{1,0:T(8,128)S(1)} %collective-permute-done.15.refs_5_), channel_id=1, source_target_pairs={{0,2},{1,3},{2,0},{3,1},{4,6},{5,7},{6,4},{7,5},{8,10},{9,11},{10,... | collective-permute-start | bytes 3145736 | tf_op jit(solution)/shard_map/ppermute | solution.py:528
  91.9 1.9 %collective-permute-start.22 = (f32[256,512]{1,0:T(8,128)S(1)}, f32[256,512]{1,0:T(8,128)S(1)}, u32[]{:S(2)}, u32[]{:S(2)}) collective-permute-start(f32[256,512]{1,0:T(8,128)S(1)} %collective-permute-done.17.refs_4_), channel_id=1, source_target_pairs={{0,4},{1,5},{2,6},{3,7},{4,0},{5,1},{6,2},{7,3},{8,12},{9,13},{10,... | collective-permute-start | bytes 1572872 | tf_op jit(solution)/shard_map/ppermute | solution.py:528
  93.9 6.6 %factor_step.5 = (f32[512,512]{1,0:T(8,128)S(1)}, f32[512,512]{1,0:T(8,128)S(1)}) custom-call(f32[512,512]{1,0:T(8,128)S(1)} %get-tuple-element.63.u_in, f32[512,512]{1,0:T(8,128)S(1)} %get-tuple-element.64.x_in), custom_call_target="tpu_custom_call" | custom-call | flops 1000000 | bytes 2048 | tf_op jit(solution)/shard_map/factor_step/pallas_call | solution.py:265
  100.5 1.6 %collective-permute-done.18.recv_hbm = f32[4096,512]{1,0:T(8,128)} collective-permute-done((f32[4096,512]{1,0:T(8,128)}, f32[4096,512]{1,0:T(8,128)}, u32[]{:S(2)}, u32[]{:S(2)}) %collective-permute-start.18) | collective-permute-done | bytes 8388640 | tf_op jit(solution)/shard_map/ppermute | solution.py:566
  102.1 19.7 %factor_and_finish.1 = (f32[4096,512]{1,0:T(8,128)}, f32[512,512]{1,0:T(8,128)S(1)}, f32[512,512]{1,0:T(8,128)S(1)}) custom-call(s32[3]{0:T(128)S(1)} %copy-done.2, s32[4,32]{1,0:T(4,128)S(1)} %pad_add_fusion.index, f32[512,512]{1,0:T(8,128)S(1)} %get-tuple-element.65.u_in, f32[512,512]{1,0:T(8,128)S(1)} %get-tuple-element.66.x_in, f32[512,512]{1,0:T(8,128)} %copy-done.1, ...), custom_call_target="tpu_custom_call" | custom-call | flops 1000000 | bytes 2048 | tf_op jit(solution)/shard_map/factor_and_finish/pallas_call | solution.py:385
  121.9 6.1 %finish.1 = f32[4096,512]{1,0:T(8,128)} custom-call(s32[3]{0:T(128)S(1)} %copy-done.2, f32[4096,512]{1,0:T(8,128)} %get-tuple-element.72.base_hbm, f32[512,512]{1,0:T(8,128)S(1)} %get-tuple-element.73.mult_ref, f32[512,512]{1,0:T(8,128)S(1)} %get-tuple-element.74.top_ref, ...), custom_call_target="tpu_custom_call", output_to_operand_aliasing={{}: (1, {})} | custom-call | flops 2415919104 | bytes 9437184 | tf_op jit(solution)/shard_map/finish/pallas_call | solution.py:439
  (62 shorter events, 20.7 us)
Async XLA Ops:
  4.1 3.0 %collective-permute-start = (f32[512,512]{1,0:T(8,128)}, f32[512,512]{1,0:T(8,128)S(1)}, u32[]{:S(2)}, u32[]{:S(2)}) collective-permute-start(f32[512,512]{1,0:T(8,128)} %pivot_rows.1.mine_ref), channel_id=1, source_target_pairs={{0,16},{16,0},{1,17},{17,1},{2,18},{18,2},{3,19},{19,3},{4,20},{20... | collective-permute-start | bytes 3145736 | tf_op jit(solution)/shard_map/ppermute | solution.py:514
  10.3 31.7 %collective-permute-start.8 = (f32[512,512]{1,0:T(8,128)S(1)}, f32[512,512]{1,0:T(8,128)S(1)}, u32[]{:S(2)}, u32[]{:S(2)}) collective-permute-start(f32[512,512]{1,0:T(8,128)S(1)} %get-tuple-element.47), channel_id=1, source_target_pairs={{0,8},{1,9},{2,10},{3,11},{4,12},{5,13},{6,14},{7,15},{24,16},{25,... | collective-permute-start | bytes 3145736 | tf_op jit(solution)/shard_map/ppermute | solution.py:518
  16.2 1.2 collective-permute-start.5
  17.6 7.2 %collective-permute-start.2 = (f32[320,128]{1,0:T(8,128)S(1)}, f32[320,128]{1,0:T(8,128)S(1)}, u32[]{:S(2)}, u32[]{:S(2)}) collective-permute-start(f32[320,128]{1,0:T(8,128)S(1)} %get-tuple-element.41), channel_id=1, source_target_pairs={{0,2},{16,18}} | collective-permute-start | bytes 491528 | tf_op jit(solution)/shard_map/ppermute | solution.py:497
  21.1 5.1 %collective-permute-start.1 = (f32[320,128]{1,0:T(8,128)S(1)}, f32[320,128]{1,0:T(8,128)S(1)}, u32[]{:S(2)}, u32[]{:S(2)}) collective-permute-start(f32[320,128]{1,0:T(8,128)S(1)} %get-tuple-element.40), channel_id=1, source_target_pairs={{0,1},{16,17}} | collective-permute-start | bytes 491528 | tf_op jit(solution)/shard_map/ppermute | solution.py:497
  26.2 7.4 %collective-permute-start.4 = (f32[320,128]{1,0:T(8,128)S(1)}, f32[320,128]{1,0:T(8,128)S(1)}, u32[]{:S(2)}, u32[]{:S(2)}) collective-permute-start(f32[320,128]{1,0:T(8,128)S(1)} %add.60), channel_id=1, source_target_pairs={{0,1},{2,3},{16,17},{18,19}} | collective-permute-start | bytes 491528 | tf_op jit(solution)/shard_map/ppermute | solution.py:497
  30.6 4.3 %collective-permute-start.3 = (f32[320,128]{1,0:T(8,128)S(1)}, f32[320,128]{1,0:T(8,128)S(1)}, u32[]{:S(2)}, u32[]{:S(2)}) collective-permute-start(f32[320,128]{1,0:T(8,128)S(1)} %add.59), channel_id=1, source_target_pairs={{0,2},{1,3},{16,18},{17,19}} | collective-permute-start | bytes 491528 | tf_op jit(solution)/shard_map/ppermute | solution.py:497
  34.9 5.3 %collective-permute-start.7 = (f32[320,128]{1,0:T(8,128)S(1)}, f32[320,128]{1,0:T(8,128)S(1)}, u32[]{:S(2)}, u32[]{:S(2)}) collective-permute-start(f32[320,128]{1,0:T(8,128)S(1)} %add.62), channel_id=1, source_target_pairs={{0,4},{2,6},{1,5},{3,7},{16,20},{18,22},{17,21},{19,23}} | collective-permute-start | bytes 491528 | tf_op jit(solution)/shard_map/ppermute | solution.py:497
  36.2 5.7 %collective-permute-start.6 = (f32[320,128]{1,0:T(8,128)S(1)}, f32[320,128]{1,0:T(8,128)S(1)}, u32[]{:S(2)}, u32[]{:S(2)}) collective-permute-start(f32[320,128]{1,0:T(8,128)S(1)} %add.61), channel_id=1, source_target_pairs={{0,4},{1,5},{2,6},{3,7},{16,20},{17,21},{18,22},{19,23}} | collective-permute-start | bytes 491528 | tf_op jit(solution)/shard_map/ppermute | solution.py:497
  42.2 40.6 %copy-start.3 = (f32[512,512]{1,0:T(8,128)}, f32[512,512]{1,0:T(8,128)S(1)}, u32[]{:S(2)}) copy-start(f32[512,512]{1,0:T(8,128)S(1)} %broadcast_select_fusion.refs_0_) | copy-start | bytes 3145732
  42.2 31.9 %collective-permute-start.13 = (f32[512,512]{1,0:T(8,128)S(1)}, f32[512,512]{1,0:T(8,128)S(1)}, u32[]{:S(2)}, u32[]{:S(2)}) collective-permute-start(f32[512,512]{1,0:T(8,128)S(1)} %broadcast_select_fusion.refs_0_), channel_id=1, source_target_pairs={{0,1},{1,0},{2,3},{3,2},{4,5},{5,4},{6,7},{7,6},{8,9},{9,8},{10,11... | collective-permute-start | bytes 3145736 | tf_op jit(solution)/shard_map/ppermute | solution.py:528
  43.6 30.5 %collective-permute-start.14 = (f32[512,512]{1,0:T(8,128)S(1)}, f32[512,512]{1,0:T(8,128)S(1)}, u32[]{:S(2)}, u32[]{:S(2)}) collective-permute-start(f32[512,512]{1,0:T(8,128)S(1)} %broadcast_select_fusion.refs_0_), channel_id=1, source_target_pairs={{0,2},{1,3},{2,0},{3,1},{4,6},{5,7},{6,4},{7,5},{8,10},{9,11},{10,... | collective-permute-start | bytes 3145736 | tf_op jit(solution)/shard_map/ppermute | solution.py:528
  45.0 4.5 %collective-permute-start.10 = (f32[320,128]{1,0:T(8,128)S(1)}, f32[320,128]{1,0:T(8,128)S(1)}, u32[]{:S(2)}, u32[]{:S(2)}) collective-permute-start(f32[320,128]{1,0:T(8,128)S(1)} %add.66), channel_id=1, source_target_pairs={{0,8},{2,10},{1,9},{3,11},{4,12},{6,14},{5,13},{7,15},{16,24},{18,... | collective-permute-start | bytes 491528 | tf_op jit(solution)/shard_map/ppermute | solution.py:497
  46.2 5.0 %collective-permute-start.9 = (f32[320,128]{1,0:T(8,128)S(1)}, f32[320,128]{1,0:T(8,128)S(1)}, u32[]{:S(2)}, u32[]{:S(2)}) collective-permute-start(f32[320,128]{1,0:T(8,128)S(1)} %add.65), channel_id=1, source_target_pairs={{0,8},{1,9},{2,10},{3,11},{4,12},{5,13},{6,14},{7,15},{16,24},{17,... | collective-permute-start | bytes 491528 | tf_op jit(solution)/shard_map/ppermute | solution.py:497
  51.2 31.8 %collective-permute-start.15 = (f32[512,512]{1,0:T(8,128)S(1)}, f32[512,512]{1,0:T(8,128)S(1)}, u32[]{:S(2)}, u32[]{:S(2)}) collective-permute-start(f32[512,512]{1,0:T(8,128)S(1)} %broadcast_select_fusion.refs_0_), channel_id=1, source_target_pairs={{0,4},{1,5},{2,6},{3,7},{4,0},{5,1},{6,2},{7,3},{8,12},{9,13},{10,... | collective-permute-start | bytes 3145736 | tf_op jit(solution)/shard_map/ppermute | solution.py:528
  59.7 1.4 %collective-permute-start.11 = (f32[320,128]{1,0:T(8,128)S(1)}, f32[320,128]{1,0:T(8,128)S(1)}, u32[]{:S(2)}, u32[]{:S(2)}) collective-permute-start(f32[320,128]{1,0:T(8,128)S(1)} %add.67.refs_0_), channel_id=1, source_target_pairs={{0,16},{16,0},{1,17},{17,1},{2,18},{18,2},{3,19},{19,3},{4,20},{20... | collective-permute-start | bytes 491528 | tf_op jit(solution)/shard_map/ppermute | solution.py:558
  59.7 1.6 %collective-permute-start.12 = (f32[320,128]{1,0:T(8,128)S(1)}, f32[320,128]{1,0:T(8,128)S(1)}, u32[]{:S(2)}, u32[]{:S(2)}) collective-permute-start(f32[320,128]{1,0:T(8,128)S(1)} %add.68.refs_1_), channel_id=1, source_target_pairs={{0,16},{16,0},{1,17},{17,1},{2,18},{18,2},{3,19},{19,3},{4,20},{20... | collective-permute-start | bytes 491528 | tf_op jit(solution)/shard_map/ppermute | solution.py:558
  74.2 14.2 %collective-permute-start.16 = (f32[256,512]{1,0:T(8,128)S(1)}, f32[256,512]{1,0:T(8,128)S(1)}, u32[]{:S(2)}, u32[]{:S(2)}) collective-permute-start(f32[256,512]{1,0:T(8,128)S(1)} %slice.6), channel_id=1, source_target_pairs={{0,2},{1,3},{2,0},{3,1},{4,6},{5,7},{6,4},{7,5},{8,10},{9,11},{10,... | collective-permute-start | bytes 1572872 | tf_op jit(solution)/shard_map/ppermute | solution.py:528
  74.7 13.9 %collective-permute-start.17 = (f32[256,512]{1,0:T(8,128)S(1)}, f32[256,512]{1,0:T(8,128)S(1)}, u32[]{:S(2)}, u32[]{:S(2)}) collective-permute-start(f32[256,512]{1,0:T(8,128)S(1)} %slice.7), channel_id=1, source_target_pairs={{0,1},{1,0},{2,3},{3,2},{4,5},{5,4},{6,7},{7,6},{8,9},{9,8},{10,11... | collective-permute-start | bytes 1572872 | tf_op jit(solution)/shard_map/ppermute | solution.py:528
  88.6 13.5 %collective-permute-start.18 = (f32[4096,512]{1,0:T(8,128)}, f32[4096,512]{1,0:T(8,128)}, u32[]{:S(2)}, u32[]{:S(2)}) collective-permute-start(f32[4096,512]{1,0:T(8,128)} %get-tuple-element.68), channel_id=1, source_target_pairs={{0,16},{16,0},{1,17},{17,1},{2,18},{18,2},{3,19},{19,3},{4,20},{20... | collective-permute-start | bytes 25165832 | tf_op jit(solution)/shard_map/ppermute | solution.py:566
  88.6 33.3 %collective-permute-start.19 = (f32[512,512]{1,0:T(8,128)S(1)}, f32[512,512]{1,0:T(8,128)S(1)}, u32[]{:S(2)}, u32[]{:S(2)}) collective-permute-start(f32[512,512]{1,0:T(8,128)S(1)} %collective-permute-done.15.refs_5_), channel_id=1, source_target_pairs={{0,1},{1,0},{2,3},{3,2},{4,5},{5,4},{6,7},{7,6},{8,9},{9,8},{10,11... | collective-permute-start | bytes 3145736 | tf_op jit(solution)/shard_map/ppermute | solution.py:528
  90.1 31.7 %collective-permute-start.20 = (f32[512,512]{1,0:T(8,128)S(1)}, f32[512,512]{1,0:T(8,128)S(1)}, u32[]{:S(2)}, u32[]{:S(2)}) collective-permute-start(f32[512,512]{1,0:T(8,128)S(1)} %collective-permute-done.15.refs_5_), channel_id=1, source_target_pairs={{0,2},{1,3},{2,0},{3,1},{4,6},{5,7},{6,4},{7,5},{8,10},{9,11},{10,... | collective-permute-start | bytes 3145736 | tf_op jit(solution)/shard_map/ppermute | solution.py:528
  91.9 30.0 %collective-permute-start.21 = (f32[256,512]{1,0:T(8,128)S(1)}, f32[256,512]{1,0:T(8,128)S(1)}, u32[]{:S(2)}, u32[]{:S(2)}) collective-permute-start(f32[256,512]{1,0:T(8,128)S(1)} %collective-permute-done.16.refs_3_), channel_id=1, source_target_pairs={{0,4},{1,5},{2,6},{3,7},{4,0},{5,1},{6,2},{7,3},{8,12},{9,13},{10,... | collective-permute-start | bytes 1572872 | tf_op jit(solution)/shard_map/ppermute | solution.py:528
  91.9 29.9 %collective-permute-start.22 = (f32[256,512]{1,0:T(8,128)S(1)}, f32[256,512]{1,0:T(8,128)S(1)}, u32[]{:S(2)}, u32[]{:S(2)}) collective-permute-start(f32[256,512]{1,0:T(8,128)S(1)} %collective-permute-done.17.refs_4_), channel_id=1, source_target_pairs={{0,4},{1,5},{2,6},{3,7},{4,0},{5,1},{6,2},{7,3},{8,12},{9,13},{10,... | collective-permute-start | bytes 1572872 | tf_op jit(solution)/shard_map/ppermute | solution.py:528
  (7 other events, 99.2 us)
